TPU v7x, 32 devices: a whole 2x2x4 slice. The times are simulated.
32 devices in a mesh: energy: 8 (over z, x), slab: 4 (over y, core).
Axes of the slice: x: 2, y: 2, z: 4, core: 2. Of those that a mesh axis runs over, the one named last changes fastest.
Arguments:
- green: float32 [64, 4, 2, 256, 256], P(('energy', 'slab')), may hold values from -6 to 6
- phonon: float32 [32, 4, 2, 128, 128], P('energy', 'slab'), may hold values from -6 to 6
- coupling: float32 [256, 128], replicated, may hold values from -0.5 to 0.5
- occupation: float32 [32], replicated, may hold values from 0.1 to 3
- shifts: int32 [32], replicated, may hold values from 1 to 8, as said below
Outputs:
- sigma: float32 [64, 4, 2, 256, 256], P(('energy', 'slab'))
- polar: float32 [32, 4, 2, 128, 128], P('energy', 'slab')
Inputs may be any that keep to these rules, and one draw needn't show every extreme that they name: `shifts`: some frequency has a shift of exactly 8.
All inputs are finite; a program needn't handle non-finite values.
Results may differ from a plain program's by a relative error of at most 0.0003.
Values sent between devices are 32-bit elements; how exact they have to be, the bound alone decides.
A program may use at most 192 MiB of HBM per device.

v0:
```python
import math

import jax
import jax.numpy as jnp
from jax import lax
from jax.sharding import PartitionSpec as P


def extended(cells, sides, width):
    for axis, dim in sides:
        count = lax.axis_size(axis)
        ends = count - 1
        head = lax.slice_in_dim(cells, 0, width, axis=dim)
        tail = lax.slice_in_dim(cells, cells.shape[dim] - width, cells.shape[dim], axis=dim)
        cells = jnp.concatenate(
            [
                lax.ppermute(tail, axis, [(i, (i + 1) % count) for i in range(ends)]),
                cells,
                lax.ppermute(head, axis, [((i + 1) % count, i) for i in range(ends)]),
            ],
            axis=dim,
        )
    return cells


def lift_blocks(coupling, blocks):
    return jnp.einsum(
        "im,...mk,jk->...ij", coupling, blocks, coupling, precision=lax.Precision.HIGHEST
    )


def lower_blocks(coupling, blocks):
    return jnp.einsum(
        "bi,...bc,cj->...ij", coupling, blocks, coupling, precision=lax.Precision.HIGHEST
    )


def shards(green, phonon, coupling, occupation, shifts):
    owned = lax.all_to_all(green, "slab", split_axis=1, concat_axis=0, tiled=True)
    e_own = owned.shape[0]
    n_energy = lax.axis_size("energy")
    window = extended(owned, (("energy", 0),), e_own)
    coupled = lift_blocks(coupling, lax.all_gather(phonon, "energy", axis=0, tiled=True))
    total_w = coupled.shape[0]
    sig_scale = 1.0 / math.sqrt(total_w)
    pol_scale = 1.0 / math.sqrt(e_own * n_energy)
    levels = jnp.arange(1, e_own + 1, dtype=jnp.int32)
    select = (shifts[None, :] == levels[:, None]).astype(jnp.float32)
    flat_coupled = coupled.reshape(total_w, -1)
    block_shape = (e_own,) + coupled.shape[1:]
    emit_table = jnp.dot(
        select * (occupation + 1.0)[None, :], flat_coupled, precision=lax.Precision.HIGHEST
    ).reshape(block_shape)
    absorb_table = jnp.dot(
        select * occupation[None, :], flat_coupled, precision=lax.Precision.HIGHEST
    ).reshape(block_shape)

    def complex_product(factor, blocks):
        real = factor[None, :, 0] * blocks[:, :, 0] - factor[None, :, 1] * blocks[:, :, 1]
        imag = factor[None, :, 0] * blocks[:, :, 1] + factor[None, :, 1] * blocks[:, :, 0]
        return (real, imag)

    def add_level(level, totals):
        distance = (level + 1).astype(jnp.int32)
        above = lax.dynamic_slice_in_dim(window, e_own + distance, e_own, 0)
        below = lax.dynamic_slice_in_dim(window, e_own - distance, e_own, 0)
        up_real, up_imag = complex_product(emit_table[level], above)
        down_real, down_imag = complex_product(absorb_table[level], below)
        return (totals[0] + up_real + down_real, totals[1] + up_imag + down_imag)

    start_sum = jnp.zeros((e_own,) + owned.shape[1:2] + owned.shape[3:], jnp.float32)
    sum_real, sum_imag = lax.fori_loop(0, e_own, add_level, (start_sum, start_sum))
    sigma_owned = jnp.stack([sum_real, sum_imag], axis=2) * sig_scale
    sigma = lax.all_to_all(sigma_owned, "slab", split_axis=0, concat_axis=1, tiled=True)

    def one_shift(shift):
        part = lax.dynamic_slice_in_dim(window, e_own + shift, e_own, 0)
        real = jnp.sum(part[:, :, 0] * owned[:, :, 0] + part[:, :, 1] * owned[:, :, 1], axis=0)
        imag = jnp.sum(part[:, :, 1] * owned[:, :, 0] - part[:, :, 0] * owned[:, :, 1], axis=0)
        return jnp.stack([real, imag], axis=1) * pol_scale

    level_pairs = lax.map(one_shift, levels)
    level_polar = lower_blocks(coupling, level_pairs)
    polar = lax.psum_scatter(
        jnp.take(level_polar, shifts - 1, axis=0), "energy", scatter_dimension=0, tiled=True
    )
    return (sigma, polar)


def solution(mesh):
    placed = (
        P(("energy", "slab"), None, None, None, None),
        P("energy", "slab", None, None, None),
        P(),
        P(),
        P(),
    )
    return jax.shard_map(
        shards,
        mesh=mesh,
        in_specs=placed,
        out_specs=(
            P(("energy", "slab"), None, None, None, None),
            P("energy", "slab", None, None, None),
        ),
        check_vma=False,
    )
```

profile of v0, /device:TPU:0, one launch (start us, length us, event | category | flops | bytes accessed | tf_op | source)
XLA Modules:
  0.0 558.4 jit_solution(16414672978302440486)
XLA Ops:
  7.2 4.6 copy.25
  11.8 4.8 all-to-all-start
  17.4 48.1 %all-to-all-done = f32[2,4,2,256,256]{4,3,2,0,1:T(8,128)} async-done(((f32[2,4,2,256,256]{4,3,2,0,1:T(8,128)}), f32[2,4,2,256,256]{4,3,2,0,1:T(8,128)}, u32[]{:S(2)}, u32[]{:S(2)}) %all-to-all-start) | async-done | bytes 4194336 | tf_op jit(solution)/shard_map/all_to_all | solution.py:39
  65.6 4.6 copy.26
  70.2 6.2 %collective-permute-start = (f32[8,1,2,256,256]{4,3,0,2,1:T(8,128)}, f32[8,1,2,256,256]{4,3,0,2,1:T(8,128)}, u32[]{:S(2)}, u32[]{:S(2)}) collective-permute-start(f32[8,1,2,256,256]{4,3,0,2,1:T(8,128)} %copy.26), channel_id=1, source_target_pairs={{0,4},{4,8},{8,12},{12,16},{16,20},{20,24},{24,28},{1,5},{5,9},{9,... | collective-permute-start | bytes 12582920 | tf_op jit(solution)/shard_map/ppermute | solution.py:17
  77.8 181.0 %collective-permute-done = f32[8,1,2,256,256]{4,3,0,2,1:T(8,128)} collective-permute-done((f32[8,1,2,256,256]{4,3,0,2,1:T(8,128)}, f32[8,1,2,256,256]{4,3,0,2,1:T(8,128)}, u32[]{:S(2)}, u32[]{:S(2)}) %collective-permute-start) | collective-permute-done | bytes 4194336 | tf_op jit(solution)/shard_map/ppermute | solution.py:17
  258.7 4.6 constant_dynamic-update-slice_fusion.2
  263.3 4.7 constant_dynamic-update-slice_fusion.1
  268.0 8.9 %fusion.7 = f32[32,2,128,256]{2,3,1,0:T(8,128)S(1)} fusion(f32[32,1,2,128,128]{4,3,2,1,0:T(8,128)} %all-gather.2.cloned.1.call-done, f32[256,128]{1,0:T(8,128)S(1)} %copy-done), kind=kOutput, calls=%fused_computation.28 | convolution fusion | flops 3221225472 | bytes 12713984 | tf_op jit(solution)/shard_map/im,...mk,jk->...ij/dot_general | solution.py:27
  276.8 15.2 %fusion.37 = f32[2,256,256,32]{2,1,0,3:T(8,128)S(1)} fusion(f32[32,2,128,256]{2,3,1,0:T(8,128)S(1)} %fusion.7, f32[256,128]{1,0:T(8,128)S(1)} %copy-done), kind=kOutput, calls=%fused_computation.63 | convolution fusion | flops 6442450944 | bytes 25296896 | tf_op jit(solution)/shard_map/im,...mk,jk->...ij/dot_general | solution.py:27
  292.1 16.8 %fusion.14 = f32[8,1,2,256,256]{4,0,3,2,1:T(8,128)} fusion(f32[2,256,256,32]{2,1,0,3:T(8,128)S(1)} %fusion.37, f32[32]{0:T(128)S(1)} %copy-done.3, s32[32]{0:T(128)S(1)} %copy-done.2, s32[8]{0:T(128)S(1)} %iota_add_fusion), kind=kOutput, calls=%fused_computation.34 | convolution fusion | flops 402653696 | bytes 20971808 | tf_op jit(solution)/shard_map/dot_general | solution.py:54
  308.9 16.8 %fusion.11 = f32[8,1,2,256,256]{4,0,3,2,1:T(8,128)} fusion(f32[2,256,256,32]{2,1,0,3:T(8,128)S(1)} %fusion.37, f32[32]{0:T(128)S(1)} %broadcast_add_fusion, s32[32]{0:T(128)S(1)} %copy-done.2, s32[8]{0:T(128)S(1)} %iota_add_fusion), kind=kOutput, calls=%fused_computation.33 | convolution fusion | flops 402653696 | bytes 20971808 | tf_op jit(solution)/shard_map/dot_general | solution.py:51
  325.6 4.6 constant_dynamic-update-slice_fusion
  330.2 56.9 %while.32 = (s32[]{:T(128)}, f32[8,1,2,256,256]{4,3,2,1,0:T(8,128)}, s32[8]{0:T(128)S(1)}, f32[24,1,2,256,256]{4,3,0,2,1:T(8,128)}, f32[8,1,2,256,256]{4,3,2,1,0...) while((s32[]{:T(128)}, f32[8,1,2,256,256]{4,3,2,1,0:T(8,128)}, s32[8]{0:T(128)S(1)}, ...), condition=%wide.region_5.6_spmd, body=%wide.region_2.5_spmd.sunk | while | flops 4325383 | bytes 9962163 | solution.py:82
  332.1 4.3 add_reduce_fusion.2
  339.2 4.3 add_reduce_fusion.2
  346.3 4.3 add_reduce_fusion.2
  353.4 4.3 add_reduce_fusion.2
  360.4 4.3 add_reduce_fusion.2
  367.5 4.3 add_reduce_fusion.2
  387.1 4.7 fusion.9
  396.3 4.8 bitcast_select_fusion
  401.2 94.5 %while.33 = (s32[]{:T(128)}, f32[8,1,256,256]{3,2,1,0:T(8,128)S(1)}, f32[8,1,256,256]{3,2,1,0:T(8,128)}, f32[8,1,2,256,256]{4,0,3,2,1:T(8,128)}, f32[24,1,2,256,...) while((s32[]{:T(128)}, ...), condition=%wide.region_1.0_spmd.clone, body=%wide.region_0.0_spmd.clone.sunk | while | flops 9437196 | bytes 24117508 | solution.py:72
  405.6 6.9 %fusion.46 = (f32[8,1,256,256]{3,2,1,0:T(8,128)}, f32[8,1,256,256]{3,2,1,0:T(8,128)S(1)}) fusion(f32[8,1,256,256]{3,2,1,0:T(8,128)} %get-tuple-element.468, f32[24,1,2,256,256]{4,3,0,2,1:T(8,128)} %get-tuple-element.483, s32[]{:T(128)S(6)} %select_n.70, s32[]{:T(128)S(6)} %select_n.71, s32[]{:T(128)S(6)} %add.314, ...), kind=kLoop, calls=%fused_computation.12.clone.1 | loop fusion | flops 9437184 | bytes 17825804 | tf_op jit(solution)/shard_map/while/body/eval_jaxpr/add | solution.py:69
  416.8 7.4 %fusion.46 = (f32[8,1,256,256]{3,2,1,0:T(8,128)}, f32[8,1,256,256]{3,2,1,0:T(8,128)S(1)}) fusion(f32[8,1,256,256]{3,2,1,0:T(8,128)} %get-tuple-element.468, f32[24,1,2,256,256]{4,3,0,2,1:T(8,128)} %get-tuple-element.483, s32[]{:T(128)S(6)} %select_n.70, s32[]{:T(128)S(6)} %select_n.71, s32[]{:T(128)S(6)} %add.314, ...), kind=kLoop, calls=%fused_computation.12.clone.1 | loop fusion | flops 9437184 | bytes 17825804 | tf_op jit(solution)/shard_map/while/body/eval_jaxpr/add | solution.py:69
  428.8 7.6 %fusion.46 = (f32[8,1,256,256]{3,2,1,0:T(8,128)}, f32[8,1,256,256]{3,2,1,0:T(8,128)S(1)}) fusion(f32[8,1,256,256]{3,2,1,0:T(8,128)} %get-tuple-element.468, f32[24,1,2,256,256]{4,3,0,2,1:T(8,128)} %get-tuple-element.483, s32[]{:T(128)S(6)} %select_n.70, s32[]{:T(128)S(6)} %select_n.71, s32[]{:T(128)S(6)} %add.314, ...), kind=kLoop, calls=%fused_computation.12.clone.1 | loop fusion | flops 9437184 | bytes 17825804 | tf_op jit(solution)/shard_map/while/body/eval_jaxpr/add | solution.py:69
  440.8 7.5 %fusion.46 = (f32[8,1,256,256]{3,2,1,0:T(8,128)}, f32[8,1,256,256]{3,2,1,0:T(8,128)S(1)}) fusion(f32[8,1,256,256]{3,2,1,0:T(8,128)} %get-tuple-element.468, f32[24,1,2,256,256]{4,3,0,2,1:T(8,128)} %get-tuple-element.483, s32[]{:T(128)S(6)} %select_n.70, s32[]{:T(128)S(6)} %select_n.71, s32[]{:T(128)S(6)} %add.314, ...), kind=kLoop, calls=%fused_computation.12.clone.1 | loop fusion | flops 9437184 | bytes 17825804 | tf_op jit(solution)/shard_map/while/body/eval_jaxpr/add | solution.py:69
  452.7 7.6 %fusion.46 = (f32[8,1,256,256]{3,2,1,0:T(8,128)}, f32[8,1,256,256]{3,2,1,0:T(8,128)S(1)}) fusion(f32[8,1,256,256]{3,2,1,0:T(8,128)} %get-tuple-element.468, f32[24,1,2,256,256]{4,3,0,2,1:T(8,128)} %get-tuple-element.483, s32[]{:T(128)S(6)} %select_n.70, s32[]{:T(128)S(6)} %select_n.71, s32[]{:T(128)S(6)} %add.314, ...), kind=kLoop, calls=%fused_computation.12.clone.1 | loop fusion | flops 9437184 | bytes 17825804 | tf_op jit(solution)/shard_map/while/body/eval_jaxpr/add | solution.py:69
  464.7 7.3 %fusion.46 = (f32[8,1,256,256]{3,2,1,0:T(8,128)}, f32[8,1,256,256]{3,2,1,0:T(8,128)S(1)}) fusion(f32[8,1,256,256]{3,2,1,0:T(8,128)} %get-tuple-element.468, f32[24,1,2,256,256]{4,3,0,2,1:T(8,128)} %get-tuple-element.483, s32[]{:T(128)S(6)} %select_n.70, s32[]{:T(128)S(6)} %select_n.71, s32[]{:T(128)S(6)} %add.314, ...), kind=kLoop, calls=%fused_computation.12.clone.1 | loop fusion | flops 9437184 | bytes 17825804 | tf_op jit(solution)/shard_map/while/body/eval_jaxpr/add | solution.py:69
  476.4 7.4 %fusion.46 = (f32[8,1,256,256]{3,2,1,0:T(8,128)}, f32[8,1,256,256]{3,2,1,0:T(8,128)S(1)}) fusion(f32[8,1,256,256]{3,2,1,0:T(8,128)} %get-tuple-element.468, f32[24,1,2,256,256]{4,3,0,2,1:T(8,128)} %get-tuple-element.483, s32[]{:T(128)S(6)} %select_n.70, s32[]{:T(128)S(6)} %select_n.71, s32[]{:T(128)S(6)} %add.314, ...), kind=kLoop, calls=%fused_computation.12.clone.1 | loop fusion | flops 9437184 | bytes 17825804 | tf_op jit(solution)/shard_map/while/body/eval_jaxpr/add | solution.py:69
  488.3 7.4 %fusion.46 = (f32[8,1,256,256]{3,2,1,0:T(8,128)}, f32[8,1,256,256]{3,2,1,0:T(8,128)S(1)}) fusion(f32[8,1,256,256]{3,2,1,0:T(8,128)} %get-tuple-element.468, f32[24,1,2,256,256]{4,3,0,2,1:T(8,128)} %get-tuple-element.483, s32[]{:T(128)S(6)} %select_n.70, s32[]{:T(128)S(6)} %select_n.71, s32[]{:T(128)S(6)} %add.314, ...), kind=kLoop, calls=%fused_computation.12.clone.1 | loop fusion | flops 9437184 | bytes 17825804 | tf_op jit(solution)/shard_map/while/body/eval_jaxpr/add | solution.py:69
  497.7 50.9 %all_to_all.36 = f32[8,1,2,256,256]{4,3,2,1,0:T(8,128)S(1)} all-to-all(f32[8,1,2,256,256]{4,3,2,1,0:T(8,128)S(1)} %maximum_multiply_fusion.1), channel_id=1, replica_groups=mesh['energy'=8,'slab'=4] {'slab'}, dimensions={0} | all-to-all | bytes 8388608 | tf_op jit(solution)/shard_map/all_to_all | solution.py:74
  (85 shorter events, 66.8 us)
Async XLA Ops:
  7.2 260.8 %copy-start = (f32[256,128]{1,0:T(8,128)S(1)}, f32[256,128]{1,0:T(8,128)}, u32[]{:S(2)}) copy-start(f32[256,128]{1,0:T(8,128)} %param.11) | copy-start | bytes 393220
  11.8 53.7 %all-to-all-start = ((f32[2,4,2,256,256]{4,3,2,0,1:T(8,128)}), f32[2,4,2,256,256]{4,3,2,0,1:T(8,128)}, u32[]{:S(2)}, u32[]{:S(2)}) async-start(f32[2,4,2,256,256]{4,3,2,0,1:T(8,128)} %copy.25), calls=%async_computation | async-start | bytes 8388608 | tf_op jit(solution)/shard_map/all_to_all | solution.py:39
  16.7 251.3 %all-gather.2.cloned.1.call-start = ((), (), s32[]{:S(2)}) async-start(), calls=%async_computation.3 | async-start | bytes 4718592 | tf_op jit(solution)/shard_map/all_gather | solution.py:43
  17.4 533.7 %reduce-scatter.2.cloned.1.call-start = ((), (), s32[]{:S(2)}) async-start(), calls=%async_computation.4 | async-start | bytes 4718592 | tf_op jit(solution)/shard_map/reduce_scatter | solution.py:84
  65.5 12.1 %copy-start.2 = (s32[32]{0:T(128)S(1)}, s32[32]{0:T(128)}, u32[]{:S(2)}) copy-start(s32[32]{0:T(128)} %param.13) | copy-start | bytes 388
  65.5 12.2 %copy-start.3 = (f32[32]{0:T(128)S(1)}, f32[32]{0:T(128)}, u32[]{:S(2)}) copy-start(f32[32]{0:T(128)} %param.12) | copy-start | bytes 388
  70.2 188.6 %collective-permute-start = (f32[8,1,2,256,256]{4,3,0,2,1:T(8,128)}, f32[8,1,2,256,256]{4,3,0,2,1:T(8,128)}, u32[]{:S(2)}, u32[]{:S(2)}) collective-permute-start(f32[8,1,2,256,256]{4,3,0,2,1:T(8,128)} %copy.26), channel_id=1, source_target_pairs={{0,4},{4,8},{8,12},{12,16},{16,20},{20,24},{24,28},{1,5},{5,9},{9,... | collective-permute-start | bytes 12582920 | tf_op jit(solution)/shard_map/ppermute | solution.py:17
  76.4 249.2 %collective-permute-start.1 = (f32[8,1,2,256,256]{4,3,0,2,1:T(8,128)}, f32[8,1,2,256,256]{4,3,0,2,1:T(8,128)}, u32[]{:S(2)}, u32[]{:S(2)}) collective-permute-start(f32[8,1,2,256,256]{4,3,0,2,1:T(8,128)} %copy.26), channel_id=1, source_target_pairs={{4,0},{8,4},{12,8},{16,12},{20,16},{24,20},{28,24},{5,1},{9,5},{13... | collective-permute-start | bytes 12582920 | tf_op jit(solution)/shard_map/ppermute | solution.py:19
  548.7 2.4 copy-start.1
Sparse Core Ops, SparseCore 0:
  19.6 169.2 all-gather.1
  401.3 89.1 reduce-scatter.1
where the time goes:
time: 566 us; the launch traced here: 558 us
  waiting for transfers between devices  230 us (41%)
  other arithmetic  107 us (19%)
  local copies, waits for them, and re-layouts  68.5 us (12%)
  matrix products  64.1 us (11%)
  blocking collectives  50.9 us (9%)
  between operations  14.6 us (3%)
  starting transfers between devices  12.4 us (2%)
  loops' own time  10.6 us (2%)
    ppermute x1, waiting for transfers between devices, extended(): lax.ppermute(tail, axis, [(i, (i + 1) % count) for i in range(ends)])  181 us
    add x8, other arithmetic, add_level(): return (totals[0] + up_real + down_real, totals[1] + up_imag + down_imag)  59.1 us
    all_to_all x1, blocking collectives, shards(): lax.all_to_all(sigma_owned, 'slab', split_axis=0, concat_axis=1, tiled=True)  50.9 us
    all_to_all x1, waiting for transfers between devices, shards(): lax.all_to_all(green, 'slab', split_axis=1, concat_axis=0, tiled=True)  48.1 us
    reduce_sum x8, other arithmetic, one_shift(): jnp.sum(part[:, :, 0] * owned[:, :, 0] + part[:, :, 1] * owned[:, :, 1],...  34.7 us
    dynamic_slice x16, local copies, waits for them, and re-layouts, add_level(): down_real, down_imag = complex_product(absorb_table[level], below)  34.2 us
    dot_general x2, matrix products, lift_blocks(): jnp.einsum('im,...mk,jk->...ij', coupling, blocks, coupling, precision=la...  24.1 us
    dot_general x1, matrix products, shards(): jnp.dot(select * occupation[None, :], flat_coupled, precision=lax.Precisi...  16.8 us
  transfers between devices with their start and end apart: 5, of which 2 were waited for; matrix products, arithmetic and copies ran while one was open for 30% of the time, Pallas kernels for 0%

commit v1 on v0

v1 whole, which is shorter than its diff:
```python
import functools
import math

import jax
import jax.numpy as jnp
from jax import lax
from jax.experimental import pallas as pl
from jax.experimental.pallas import tpu as pltpu
from jax.sharding import PartitionSpec as P

TILE = 8
LANES = 128
BLOCK = 4


def cell_of(low_ref, own_ref, high_ref):
    margin, count = low_ref.shape[0] if low_ref is not None else 0, own_ref.shape[0]

    def get(e, part, columns):
        if e < 0:
            return low_ref[e + margin, part, :, columns]
        if e >= count:
            return high_ref[e - count, part, :, columns]
        return own_ref[e, part, :, columns]

    return get


def sigma_kernel(low_ref, own_ref, high_ref, table_ref, out_ref):
    count, levels, width = own_ref.shape[0], high_ref.shape[0], own_ref.shape[3]
    get = cell_of(low_ref, own_ref, high_ref)
    for start in range(0, width, LANES):
        columns = slice(start, start + LANES)
        for first in range(0, count, BLOCK):
            block = range(first, min(first + BLOCK, count))
            real, imag = {}, {}
            for level in range(levels):
                for kind, step in ((0, level + 1), (1, -level - 1)):
                    c_re = table_ref[kind * levels + level, 0, :, columns]
                    c_im = table_ref[kind * levels + level, 1, :, columns]
                    for e in block:
                        g_re, g_im = get(e + step, 0, columns), get(e + step, 1, columns)
                        re = c_re * g_re - c_im * g_im
                        im = c_re * g_im + c_im * g_re
                        real[e] = real[e] + re if e in real else re
                        imag[e] = imag[e] + im if e in imag else im
            for e in block:
                out_ref[e, 0, :, columns] = real[e]
                out_ref[e, 1, :, columns] = imag[e]


def pairs_kernel(scale, own_ref, high_ref, out_ref):
    count, levels, width = own_ref.shape[0], high_ref.shape[0], own_ref.shape[3]
    get = cell_of(None, own_ref, high_ref)
    for start in range(0, width, LANES):
        columns = slice(start, start + LANES)
        for first in range(0, levels, BLOCK):
            block = range(first, min(first + BLOCK, levels))
            real, imag = {}, {}
            for e in range(count):
                o_re, o_im = get(e, 0, columns), get(e, 1, columns)
                for level in block:
                    p_re, p_im = get(e + level + 1, 0, columns), get(e + level + 1, 1, columns)
                    re = p_re * o_re + p_im * o_im
                    im = p_im * o_re - p_re * o_im
                    real[level] = real[level] + re if level in real else re
                    imag[level] = imag[level] + im if level in imag else im
            for level in block:
                out_ref[level, 0, :, columns] = real[level] * scale
                out_ref[level, 1, :, columns] = imag[level] * scale


def tiled(body, outer, *arrays):
    rows, width = arrays[0].shape[2:]

    def spec(n):
        return pl.BlockSpec((n, 2, TILE, width), lambda r: (0, 0, r, 0))

    moved = sum(a.size for a in arrays) + outer * 2 * rows * width
    return pl.pallas_call(
        body,
        grid=(rows // TILE,),
        in_specs=[spec(a.shape[0]) for a in arrays],
        out_specs=spec(outer),
        out_shape=jax.ShapeDtypeStruct((outer, 2, rows, width), jnp.float32),
        compiler_params=pltpu.CompilerParams(vmem_limit_bytes=32 * 1024 * 1024),
        cost_estimate=pl.CostEstimate(flops=16 * moved, bytes_accessed=4 * moved, transcendentals=0),
    )(*arrays)


def shards(green, phonon, coupling, occupation, shifts):
    n_energy, n_slab = lax.axis_size("energy"), lax.axis_size("slab")
    own, slabs, _, size, _ = green.shape
    halves = 2 if n_energy % 2 == 0 else 1
    team = halves * n_slab
    groups = [list(range(k, k + team)) for k in range(0, n_energy * n_slab, team)]
    both = ("energy", "slab")
    rows = size // halves
    levels = own * n_slab
    total_e = own * n_slab * n_energy

    every = lax.all_gather(phonon, "energy", axis=0, tiled=True)
    total_w = every.shape[0]

    pieces = green.reshape(own, slabs, 2, halves, rows, size).transpose(3, 1, 0, 2, 4, 5)
    pieces = pieces.reshape(team * own, 2, rows, size)
    mine = lax.all_to_all(pieces, both, 0, 0, axis_index_groups=groups, tiled=True)

    up = [(i, i + halves) for i in range(n_energy - halves)]
    down = [(i + halves, i) for i in range(n_energy - halves)]
    high = lax.ppermute(mine[:levels], "energy", down)
    low = lax.ppermute(mine[-levels:], "energy", up)

    share = lax.rem(lax.axis_index("energy"), halves) * rows
    my_coupling = lax.dynamic_slice_in_dim(coupling, share, rows, 0)

    steps = jnp.arange(1, levels + 1, dtype=jnp.int32)
    select = (shifts[None, :] == steps[:, None]).astype(jnp.float32) / math.sqrt(total_w)
    weights = jnp.concatenate([select * (occupation + 1.0)[None, :], select * occupation[None, :]], axis=0)
    mixed = jnp.dot(weights, every.reshape(total_w, -1), precision=lax.Precision.HIGHEST)
    mixed = mixed.reshape(2 * levels, 2, *every.shape[3:])
    half = jnp.einsum("im,lpmk->lpik", my_coupling, mixed, precision=lax.Precision.HIGH)
    tables = jnp.einsum("lpik,jk->lpij", half, coupling, precision=lax.Precision.HIGH)

    pairs = tiled(functools.partial(pairs_kernel, 1.0 / math.sqrt(total_e)), levels, mine, high)
    right = jnp.einsum("lpbc,cj->lpbj", pairs, coupling, precision=lax.Precision.HIGH)
    part = jnp.einsum("bi,lpbj->lpij", my_coupling, right, precision=lax.Precision.HIGH)
    total = lax.psum(part, "energy")
    own_w = phonon.shape[0]
    my_shifts = lax.dynamic_slice_in_dim(shifts, lax.axis_index("energy") * own_w, own_w, 0)
    chosen = (my_shifts[:, None] == steps[None, :])[:, :, None, None, None]
    polar = jnp.sum(jnp.where(chosen, total[None], 0.0), axis=1)[:, None]

    sigma_mine = tiled(sigma_kernel, team * own, low, mine, high, tables)
    back = lax.all_to_all(sigma_mine, both, 0, 0, axis_index_groups=groups, tiled=True)
    back = back.reshape(halves, slabs, own, 2, rows, size).transpose(2, 1, 3, 0, 4, 5)
    return (back.reshape(green.shape), polar)


def solution(mesh):
    placed = (
        P(("energy", "slab"), None, None, None, None),
        P("energy", "slab", None, None, None),
        P(),
        P(),
        P(),
    )
    return jax.shard_map(
        shards,
        mesh=mesh,
        in_specs=placed,
        out_specs=(
            P(("energy", "slab"), None, None, None, None),
            P("energy", "slab", None, None, None),
        ),
        check_vma=False,
    )
```

time: 566 us -> 279 us (0.49); the launches traced: 558 us -> 279 us
  waiting for transfers between devices: 230 us -> 123 us
  other arithmetic: 107 us -> 1.44 us
  matrix products: 64.1 us -> 11.6 us
  local copies, waits for them, and re-layouts: 68.5 us -> 21.6 us
  blocking collectives: 50.9 us -> 77.2 us
  Pallas kernels: 0 us -> 17.9 us
  loops' own time: 10.6 us -> 0 us
    ppermute x2, waiting for transfers between devices: 181 us -> 24.6 us  [the longest x1 24.6 us: shards(): high = lax.ppermute(mine[:levels], 'energy', down)]
    psum x0 -> x1, waiting for transfers between devices: none -> 83.9 us  [shards(): total = lax.psum(part, 'energy')]
    add x10 -> x1, other arithmetic: 59.1 us -> 0.01 us  [shards(): steps = jnp.arange(1, levels + 1, dtype=jnp.int32)]
    dot_general x6 -> x5, matrix products: 64.1 us -> 11.6 us  [the longest x1 4.4 us: shards(): jnp.dot(weights, every.reshape(total_w, -1), precision=lax.Precision.HIGH...]
    all_to_all x1, waiting for transfers between devices: 48.1 us -> 0.01 us  [shards(): lax.all_to_all(sigma_mine, both, 0, 0, axis_index_groups=groups, tiled=True)]
    dynamic_slice x32 -> x1, local copies, waits for them, and re-layouts: 39.7 us -> 0.08 us  [shards(): lax.dynamic_slice_in_dim(shifts, lax.axis_index('energy') * own_w, own_w, 0)]
    reduce_sum x8 -> x1, other arithmetic: 34.7 us -> 1.28 us  [shards(): polar = jnp.sum(jnp.where(chosen, total[None], 0.0), axis=1)[:, None]]
    all_to_all x1, blocking collectives: 50.9 us -> 77.2 us  [shards(): lax.all_to_all(pieces, both, 0, 0, axis_index_groups=groups, tiled=True)]
  transfers between devices with their start and end apart: 5 -> 5, of which waited for: 2 -> 3; matrix products, arithmetic and copies ran while one was open for 30% -> 9% of each run, Pallas kernels for 0% -> 2%
where the time goes in v1:
time: 279 us
  waiting for transfers between devices  123 us (44%)
  blocking collectives  77.2 us (28%)
  local copies, waits for them, and re-layouts  21.6 us (8%)
  Pallas kernels  17.9 us (6%)
  between operations  14.2 us (5%)
  starting transfers between devices  11.8 us (4%)
  matrix products  11.6 us (4%)
    psum x1, waiting for transfers between devices, shards(): total = lax.psum(part, 'energy')  83.9 us
    all_to_all x1, blocking collectives, shards(): lax.all_to_all(pieces, both, 0, 0, axis_index_groups=groups, tiled=True)  77.2 us
    ppermute x1, waiting for transfers between devices, shards(): high = lax.ppermute(mine[:levels], 'energy', down)  24.6 us
    pallas_call x2, Pallas kernels, tiled(): pl.pallas_call(body, grid=(rows // TILE,), in_specs=[spec(a.shape[0]) for...  17.9 us
    all_gather x1, waiting for transfers between devices, shards(): every = lax.all_gather(phonon, 'energy', axis=0, tiled=True)  13.9 us
    unnamed x16, local copies, waits for them, and re-layouts  10.2 us
    ppermute x1, starting transfers between devices, shards(): low = lax.ppermute(mine[-levels:], 'energy', up)  5.92 us
  transfers between devices with their start and end apart: 5, of which 3 were waited for; matrix products, arithmetic and copies ran while one was open for 9% of the time, Pallas kernels for 2%

profile of v1, /device:TPU:0, one launch (start us, length us, event | category | flops | bytes accessed | tf_op | source)
XLA Modules:
  0.0 278.8 jit_solution(9363897471820260517)
XLA Ops:
  7.2 0.0 copy-start
  7.2 0.0 all-gather.2.cloned.1.call-start
  7.2 0.7 all-gather.2.cloned.1.call-update
  7.9 2.5 copy.20
  10.5 77.2 %all_to_all.10.own_ref = f32[16,2,128,256]{3,2,1,0:T(8,128)S(1)} all-to-all(f32[16,2,128,256]{3,2,1,0:T(8,128)S(1)} %bitcast.51), channel_id=1, replica_groups={{0,1,2,3,4,5,6,7},{8,9,10,11,12,13,14,15},{16,17,18,19,20,21,22,23},{24..., dimensions={0} | all-to-all | bytes 8388608 | tf_op jit(solution)/shard_map/all_to_all | solution.py:107
  87.7 2.6 fusion.19
  90.3 0.7 copy-done.1
  91.0 1.3 collective-permute-start.1
  92.3 5.9 %collective-permute-start = (f32[8,2,128,256]{3,2,1,0:T(8,128)}, f32[8,2,128,256]{3,2,1,0:T(8,128)}, u32[]{:S(2)}, u32[]{:S(2)}) collective-permute-start(f32[8,2,128,256]{3,2,1,0:T(8,128)} %get-tuple-element.7), channel_id=1, source_target_pairs={{0,8},{4,12},{8,16},{12,20},{16,24},{20,28},{1,9},{5,13},{9,17},{1... | collective-permute-start | bytes 6291464 | tf_op jit(solution)/shard_map/ppermute | solution.py:112
  98.2 0.1 compare_select_fusion.1
  98.3 13.9 %all-gather.2.cloned.1.call-done = f32[32,1,2,128,128]{4,3,2,1,0:T(8,128)} async-done(((f32[4,1,2,128,128]{4,3,2,1,0:T(8,128)}), f32[32,1,2,128,128]{4,3,2,1,0:T(8,128)}) %all-gather.2.cloned.1.call-update) | async-done | bytes 4194320 | tf_op jit(solution)/shard_map/all_gather | solution.py:102
  112.2 4.6 %copy.40 = f32[4,8,256,128]{3,1,2,0:T(8,128)S(1)} copy(f32[4,8,256,128]{3,2,1,0:T(8,128)} %bitcast.53) | data formatting | bytes 8388608
  116.8 0.7 copy.34
  117.6 4.4 %fusion = f32[16,2,128,128]{3,0,2,1:T(8,128)S(1)} fusion(f32[2,128,128,32]{2,1,0,3:T(8,128)S(1)} %bitcast.50, f32[8,32]{1,0:T(8,128)S(1)} %get-tuple-element.9, f32[8,32]{1,0:T(8,128)S(1)} %get-tuple-element.8), kind=kOutput, calls=%fused_computation.1 | convolution fusion | flops 201327104 | bytes 6293504 | tf_op jit(solution)/shard_map/dot_general | solution.py:120
  122.0 2.3 fusion.4
  124.3 2.1 fusion.2.table_ref
  126.4 24.6 %collective-permute-done.1.high_ref = f32[8,2,128,256]{3,2,1,0:T(8,128)S(1)} collective-permute-done((f32[8,2,128,256]{3,2,1,0:T(8,128)}, f32[8,2,128,256]{3,2,1,0:T(8,128)S(1)}, u32[]{:S(2)}, u32[]{:S(2)}) %collective-permute-start.1) | collective-permute-done | bytes 2097184 | tf_op jit(solution)/shard_map/ppermute | solution.py:111
  151.0 12.6 %shard_map.68 = f32[16,2,128,256]{3,2,1,0:T(8,128)S(1)} custom-call(f32[8,2,128,256]{3,2,1,0:T(8,128)} %collective-permute-done.low_ref, f32[16,2,128,256]{3,2,1,0:T(8,128)S(1)} %copy-done.2, f32[8,2,128,256]{3,2,1,0:T(8,128)S(1)} %collective-permute-done.1.high_ref, f32[16,2,128,256]{3,2,1,0:T(8,128)S(1)} %fusion.2.table_ref), custom_call_target="tpu_custom_call" | custom-call | flops 67108864 | bytes 16777216 | tf_op jit(solution)/shard_map/pallas_call | solution.py:80
  163.7 2.0 copy-done.4
  165.6 4.6 %all-to-all-start.1 = ((f32[16,2,128,256]{3,2,1,0:T(8,128)}), f32[16,2,128,256]{3,2,1,0:T(8,128)}, u32[]{:S(2)}, u32[]{:S(2)}) async-start(f32[16,2,128,256]{3,2,1,0:T(8,128)} %copy-done.4), calls=%async_computation.1 | async-start | bytes 8388608 | tf_op jit(solution)/shard_map/all_to_all | solution.py:135
  170.2 0.0 all-reduce.2.cloned.1.call-start
  170.3 2.2 copy-done.3
  172.4 5.2 %shard_map.69 = f32[8,2,128,256]{3,2,1,0:T(8,128)S(1)} custom-call(f32[16,2,128,256]{3,2,1,0:T(8,128)S(1)} %copy-done.3, f32[8,2,128,256]{3,2,1,0:T(8,128)S(1)} %collective-permute-done.1.high_ref), custom_call_target="tpu_custom_call" | custom-call | flops 33554432 | bytes 8388608 | tf_op jit(solution)/shard_map/pallas_call | solution.py:80
  177.7 1.2 fusion.6
  178.9 1.6 convolution_bitcast_fusion
  180.4 0.0 all-reduce.2.cloned.1.call-update
  180.4 0.1 dynamic_slice.7
  180.5 0.1 broadcast_compare_fusion
  180.6 83.9 %all-reduce.2.cloned.1.call-done = f32[8,2,128,128]{2,3,1,0:T(8,128)} async-done(((f32[8,2,128,128]{2,3,1,0:T(8,128)}), f32[8,2,128,128]{2,3,1,0:T(8,128)}) %all-reduce.2.cloned.1.call-update) | async-done | bytes 1048592 | tf_op jit(solution)/shard_map/psum | solution.py:128
  264.5 1.6 copy.26
  266.0 1.3 select_reduce_fusion
  267.3 4.7 %copy.24 = f32[2,4,2,2,128,256]{5,4,3,2,1,0:T(8,128)} copy(f32[2,4,2,2,128,256]{5,4,2,0,1,3:T(8,128)} %bitcast.12) | data formatting | bytes 8388608 | tf_op jit(solution)/shard_map/transpose | solution.py:136
  (14 shorter events, 0.0 us)
Async XLA Ops:
  7.2 114.8 %copy-start = (f32[256,128]{1,0:T(8,128)S(1)}, f32[256,128]{1,0:T(8,128)}, u32[]{:S(2)}) copy-start(f32[256,128]{1,0:T(8,128)} %param.7) | copy-start | bytes 393220
  7.2 105.0 %all-gather.2.cloned.1.call-start = ((), (), s32[]{:S(2)}) async-start(), calls=%async_computation.2 | async-start | bytes 4718592 | tf_op jit(solution)/shard_map/all_gather | solution.py:102
  87.7 3.3 %copy-start.1 = (f32[16,2,128,256]{3,2,1,0:T(8,128)}, f32[16,2,128,256]{3,2,1,0:T(8,128)S(1)}, u32[]{:S(2)}) copy-start(f32[16,2,128,256]{3,2,1,0:T(8,128)S(1)} %all_to_all.10.own_ref) | copy-start | bytes 12582916
  87.7 10.5 %copy-start.5 = (f32[32]{0:T(128)S(1)}, f32[32]{0:T(128)}, u32[]{:S(2)}) copy-start(f32[32]{0:T(128)} %param.8) | copy-start | bytes 388
  87.7 10.5 %copy-start.6 = (s32[32]{0:T(128)S(1)}, s32[32]{0:T(128)}, u32[]{:S(2)}) copy-start(s32[32]{0:T(128)} %param.9) | copy-start | bytes 388
  91.0 60.0 %collective-permute-start.1 = (f32[8,2,128,256]{3,2,1,0:T(8,128)}, f32[8,2,128,256]{3,2,1,0:T(8,128)S(1)}, u32[]{:S(2)}, u32[]{:S(2)}) collective-permute-start(f32[8,2,128,256]{3,2,1,0:T(8,128)} %get-tuple-element.6), channel_id=1, source_target_pairs={{8,0},{12,4},{16,8},{20,12},{24,16},{28,20},{9,1},{13,5},{17,9},{2... | collective-permute-start | bytes 6291464 | tf_op jit(solution)/shard_map/ppermute | solution.py:111
  92.3 58.7 %collective-permute-start = (f32[8,2,128,256]{3,2,1,0:T(8,128)}, f32[8,2,128,256]{3,2,1,0:T(8,128)}, u32[]{:S(2)}, u32[]{:S(2)}) collective-permute-start(f32[8,2,128,256]{3,2,1,0:T(8,128)} %get-tuple-element.7), channel_id=1, source_target_pairs={{0,8},{4,12},{8,16},{12,20},{16,24},{20,28},{1,9},{5,13},{9,17},{1... | collective-permute-start | bytes 6291464 | tf_op jit(solution)/shard_map/ppermute | solution.py:112
  124.3 26.7 %copy-start.2 = (f32[16,2,128,256]{3,2,1,0:T(8,128)S(1)}, f32[16,2,128,256]{3,2,1,0:T(8,128)}, u32[]{:S(2)}) copy-start(f32[16,2,128,256]{3,2,1,0:T(8,128)} %copy-done.1) | copy-start | bytes 12582916
  163.7 2.0 copy-start.4
  165.6 101.7 %all-to-all-start.1 = ((f32[16,2,128,256]{3,2,1,0:T(8,128)}), f32[16,2,128,256]{3,2,1,0:T(8,128)}, u32[]{:S(2)}, u32[]{:S(2)}) async-start(f32[16,2,128,256]{3,2,1,0:T(8,128)} %copy-done.4), calls=%async_computation.1 | async-start | bytes 8388608 | tf_op jit(solution)/shard_map/all_to_all | solution.py:135
  170.2 94.3 %all-reduce.2.cloned.1.call-start = ((), (), s32[]{:S(2)}) async-start(), calls=%async_computation.3 | async-start | bytes 2097152 | tf_op jit(solution)/shard_map/psum | solution.py:128
  170.2 2.2 copy-start.3
Sparse Core Ops, SparseCore 0:
  10.1 101.9 all-gather.1
  180.6 83.8 all-reduce.1

commit v2 on v1

--- a/solution.py
+++ b/solution.py
@@ -99,8 +99,13 @@
     levels = own * n_slab
     total_e = own * n_slab * n_energy
 
-    every = lax.all_gather(phonon, "energy", axis=0, tiled=True)
-    total_w = every.shape[0]
+    turns = n_energy // halves
+    column = lax.rem(lax.axis_index("energy"), halves)
+    lines = [[x + halves * z for z in range(turns)] for x in range(halves)]
+    swap = [(i, i ^ 1) for i in range(n_energy)]
+    every = lax.all_gather(phonon, "energy", axis=0, axis_index_groups=lines, tiled=True)
+    own_w = phonon.shape[0]
+    total_w = own_w * n_energy
 
     pieces = green.reshape(own, slabs, 2, halves, rows, size).transpose(3, 1, 0, 2, 4, 5)
     pieces = pieces.reshape(team * own, 2, rows, size)
@@ -108,30 +113,49 @@
 
     up = [(i, i + halves) for i in range(n_energy - halves)]
     down = [(i + halves, i) for i in range(n_energy - halves)]
-    high = lax.ppermute(mine[:levels], "energy", down)
-    low = lax.ppermute(mine[-levels:], "energy", up)
 
-    share = lax.rem(lax.axis_index("energy"), halves) * rows
-    my_coupling = lax.dynamic_slice_in_dim(coupling, share, rows, 0)
+    my_coupling = lax.dynamic_slice_in_dim(coupling, column * rows, rows, 0)
 
     steps = jnp.arange(1, levels + 1, dtype=jnp.int32)
     select = (shifts[None, :] == steps[:, None]).astype(jnp.float32) / math.sqrt(total_w)
     weights = jnp.concatenate([select * (occupation + 1.0)[None, :], select * occupation[None, :]], axis=0)
-    mixed = jnp.dot(weights, every.reshape(total_w, -1), precision=lax.Precision.HIGHEST)
+    weights = weights.reshape(2 * levels, turns, halves, own_w)
+    weights = lax.dynamic_index_in_dim(weights, column, 2, keepdims=False).reshape(2 * levels, -1)
+    mixed = jnp.dot(weights, every.reshape(turns * own_w, -1), precision=lax.Precision.HIGHEST)
     mixed = mixed.reshape(2 * levels, 2, *every.shape[3:])
+    mine, mixed = lax.optimization_barrier((mine, mixed))
+    high = lax.ppermute(mine[:levels], "energy", down)
+    low = lax.ppermute(mine[-levels:], "energy", up)
+    if halves == 2:
+        mixed = mixed + lax.ppermute(mixed, "energy", swap)
     half = jnp.einsum("im,lpmk->lpik", my_coupling, mixed, precision=lax.Precision.HIGH)
     tables = jnp.einsum("lpik,jk->lpij", half, coupling, precision=lax.Precision.HIGH)
 
     pairs = tiled(functools.partial(pairs_kernel, 1.0 / math.sqrt(total_e)), levels, mine, high)
     right = jnp.einsum("lpbc,cj->lpbj", pairs, coupling, precision=lax.Precision.HIGH)
     part = jnp.einsum("bi,lpbj->lpij", my_coupling, right, precision=lax.Precision.HIGH)
-    total = lax.psum(part, "energy")
-    own_w = phonon.shape[0]
-    my_shifts = lax.dynamic_slice_in_dim(shifts, lax.axis_index("energy") * own_w, own_w, 0)
-    chosen = (my_shifts[:, None] == steps[None, :])[:, :, None, None, None]
-    polar = jnp.sum(jnp.where(chosen, total[None], 0.0), axis=1)[:, None]
+    low, part = lax.optimization_barrier((low, part))
+    modes = part.shape[2] // halves
+    kept = lax.dynamic_slice_in_dim(part, column * modes, modes, 2)
+    if halves == 2:
+        sent = lax.dynamic_slice_in_dim(part, (1 - column) * modes, modes, 2)
+        kept = kept + lax.ppermute(sent, "energy", swap)
+    sigma_mine = tiled(sigma_kernel, team * own, low, mine, high, tables)
+    sigma_mine, kept = lax.optimization_barrier((sigma_mine, kept))
+    total = lax.psum(kept, "energy", axis_index_groups=lines)
 
-    sigma_mine = tiled(sigma_kernel, team * own, low, mine, high, tables)
+    def chosen(holder):
+        own_shifts = lax.dynamic_slice_in_dim(shifts, holder * own_w, own_w, 0)
+        taken = (own_shifts[:, None] == steps[None, :])[:, :, None, None, None]
+        return jnp.sum(jnp.where(taken, total[None], 0.0), axis=1)
+
+    polar = chosen(lax.axis_index("energy"))
+    if halves == 2:
+        other = lax.ppermute(chosen(lax.axis_index("energy") + 1 - 2 * column), "energy", swap)
+        first, second = jnp.where(column == 0, polar, other), jnp.where(column == 0, other, polar)
+        polar = jnp.concatenate([first, second], axis=2)
+    polar = polar[:, None]
+
     back = lax.all_to_all(sigma_mine, both, 0, 0, axis_index_groups=groups, tiled=True)
     back = back.reshape(halves, slabs, own, 2, rows, size).transpose(2, 1, 3, 0, 4, 5)
     return (back.reshape(green.shape), polar)

time: 279 us -> 255 us (0.914)
  blocking collectives: 77.2 us -> 0 us
  waiting for transfers between devices: 123 us -> 152 us
  starting transfers between devices: 11.8 us -> 21.6 us
  Pallas kernels: 17.9 us -> 24 us
  local copies, waits for them, and re-layouts: 21.6 us -> 26.2 us
  other arithmetic: 1.44 us -> 5.47 us
    all_to_all x1 -> x0, blocking collectives: 77.2 us -> none  [shards(): lax.all_to_all(pieces, both, 0, 0, axis_index_groups=groups, tiled=True)]
    all_gather x1, waiting for transfers between devices: 13.9 us -> 49.6 us  [shards(): lax.all_gather(phonon, 'energy', axis=0, axis_index_groups=lines, tiled=T...]
    psum x1, waiting for transfers between devices: 83.9 us -> 53.2 us  [shards(): total = lax.psum(kept, 'energy', axis_index_groups=lines)]
    ppermute x1, waiting for transfers between devices: 24.6 us -> 40.8 us  [shards(): high = lax.ppermute(mine[:levels], 'energy', down)]
    ppermute x0 -> x3, waiting for transfers between devices: none -> 6.8 us  [the longest x1 6.79 us: shards(): lax.ppermute(chosen(lax.axis_index('energy') + 1 - 2 * column), 'energy',...]
    pallas_call x2, Pallas kernels: 17.9 us -> 24 us  [tiled(): pl.pallas_call(body, grid=(rows // TILE,), in_specs=[spec(a.shape[0]) for...]
    all_to_all x0 -> x1, starting transfers between devices: none -> 5.3 us  [shards(): lax.all_to_all(pieces, both, 0, 0, axis_index_groups=groups, tiled=True)]
    unnamed x16 -> x10, local copies, waits for them, and re-layouts: 10.2 us -> 5.24 us
  transfers between devices with their start and end apart: 5 -> 9, of which waited for: 3 -> 4; matrix products, arithmetic and copies ran while one was open for 9% -> 9% of each run, Pallas kernels for 2% -> 9%
where the time goes in v2:
time: 255 us; the launch traced here: 254 us
  waiting for transfers between devices  152 us (60%)
  local copies, waits for them, and re-layouts  26.2 us (10%)
  Pallas kernels  24 us (9%)
  starting transfers between devices  21.6 us (8%)
  between operations  14.2 us (6%)
  matrix products  10.2 us (4%)
  other arithmetic  5.47 us (2%)
    psum x1, waiting for transfers between devices, shards(): total = lax.psum(kept, 'energy', axis_index_groups=lines)  53.2 us
    all_gather x1, waiting for transfers between devices, shards(): lax.all_gather(phonon, 'energy', axis=0, axis_index_groups=lines, tiled=T...  49.6 us
    ppermute x1, waiting for transfers between devices, shards(): high = lax.ppermute(mine[:levels], 'energy', down)  40.8 us
    pallas_call x2, Pallas kernels, tiled(): pl.pallas_call(body, grid=(rows // TILE,), in_specs=[spec(a.shape[0]) for...  24 us
    ppermute x1, waiting for transfers between devices, shards(): lax.ppermute(chosen(lax.axis_index('energy') + 1 - 2 * column), 'energy',...  6.79 us
    ppermute x1, starting transfers between devices, shards(): low = lax.ppermute(mine[-levels:], 'energy', up)  5.91 us
    all_to_all x1, starting transfers between devices, shards(): lax.all_to_all(pieces, both, 0, 0, axis_index_groups=groups, tiled=True)  5.3 us
    unnamed x10, local copies, waits for them, and re-layouts  5.24 us
  transfers between devices with their start and end apart: 9, of which 4 were waited for; matrix products, arithmetic and copies ran while one was open for 9% of the time, Pallas kernels for 9%

profile of v2, /device:TPU:0, one launch (start us, length us, event | category | flops | bytes accessed | tf_op | source)
XLA Modules:
  0.0 253.5 jit_solution(15526527530198570938)
XLA Ops:
  7.2 4.7 %copy.34 = f32[2,4,2,2,128,256]{5,4,2,0,1,3:T(8,128)} copy(f32[2,4,2,2,128,256]{5,4,3,2,1,0:T(8,128)} %bitcast.52) | data formatting | bytes 8388608 | tf_op jit(solution)/shard_map/reshape | solution.py:110
  11.9 5.3 %all-to-all-start = ((f32[16,2,128,256]{3,2,1,0:T(8,128)}), f32[16,2,128,256]{3,2,1,0:T(8,128)}, u32[]{:S(2)}, u32[]{:S(2)}) async-start(f32[16,2,128,256]{3,2,1,0:T(8,128)} %bitcast.50), calls=%async_computation | async-start | bytes 8388608 | tf_op jit(solution)/shard_map/all_to_all | solution.py:112
  17.2 0.7 all-gather.2.cloned.1.call-update
  18.4 49.6 %all-gather.2.cloned.1.call-done = f32[16,1,2,128,128]{4,3,2,1,0:T(8,128)} async-done(((f32[4,1,2,128,128]{4,3,2,1,0:T(8,128)}), f32[16,1,2,128,128]{4,3,2,1,0:T(8,128)}) %all-gather.2.cloned.1.call-update) | async-done | bytes 2097168 | tf_op jit(solution)/shard_map/all_gather | solution.py:106
  68.0 2.8 %copy.61 = f32[2,8,256,128]{3,1,2,0:T(8,128)S(1)} copy(f32[2,8,256,128]{3,2,1,0:T(8,128)} %bitcast.54) | data formatting | bytes 4194304
  71.2 4.2 %fusion.4 = f32[16,2,128,128]{3,0,2,1:T(8,128)} fusion(f32[16,16,1,1]{0,1,3,2:T(8,128)S(1)} %bitcast.55, f32[2,128,128,16]{2,1,0,3:T(8,128)S(1)} %bitcast.51), kind=kOutput, calls=%fused_computation.5 | convolution fusion | flops 100663296 | bytes 4195328 | tf_op jit(solution)/shard_map/dot_general | solution.py:124
  75.4 4.7 %fusion.17 = (f32[8,2,128,256]{3,2,1,0:T(8,128)}, f32[8,2,128,256]{3,2,1,0:T(8,128)}) fusion(f32[16,2,128,256]{3,2,1,0:T(8,128)} %all-to-all-done.own_ref), kind=kLoop, calls=%fused_computation.34 | loop fusion | bytes 8388608 | tf_op jit(solution)/shard_map/slice | solution.py:127
  80.1 1.3 collective-permute-start.1
  81.4 5.9 %collective-permute-start = (f32[8,2,128,256]{3,2,1,0:T(8,128)}, f32[8,2,128,256]{3,2,1,0:T(8,128)}, u32[]{:S(2)}, u32[]{:S(2)}) collective-permute-start(f32[8,2,128,256]{3,2,1,0:T(8,128)} %get-tuple-element.19), channel_id=1, source_target_pairs={{0,8},{4,12},{8,16},{12,20},{16,24},{20,28},{1,9},{5,13},{9,17},{1... | collective-permute-start | bytes 6291464 | tf_op jit(solution)/shard_map/ppermute | solution.py:128
  87.3 1.5 collective-permute-start.2
  88.8 40.8 %collective-permute-done.1.high_ref = f32[8,2,128,256]{3,2,1,0:T(8,128)S(1)} collective-permute-done((f32[8,2,128,256]{3,2,1,0:T(8,128)}, f32[8,2,128,256]{3,2,1,0:T(8,128)S(1)}, u32[]{:S(2)}, u32[]{:S(2)}) %collective-permute-start.1) | collective-permute-done | bytes 2097184 | tf_op jit(solution)/shard_map/ppermute | solution.py:127
  129.6 10.4 %shard_map.68 = f32[8,2,128,256]{3,2,1,0:T(8,128)S(1)} custom-call(f32[16,2,128,256]{3,2,1,0:T(8,128)} %all-to-all-done.own_ref, f32[8,2,128,256]{3,2,1,0:T(8,128)S(1)} %collective-permute-done.1.high_ref), custom_call_target="tpu_custom_call" | custom-call | flops 33554432 | bytes 8388608 | tf_op jit(solution)/shard_map/pallas_call | solution.py:80
  140.0 1.2 fusion.7
  141.2 0.6 convolution_bitcast_fusion
  141.8 1.3 constant_dynamic-slice_fusion
  143.1 2.3 copy.43
  145.4 1.5 collective-permute-start.3
  146.9 2.5 add.56
  149.4 2.3 fusion.2
  151.7 1.9 fusion.table_ref
  153.7 13.7 %shard_map.69 = f32[16,2,128,256]{3,2,1,0:T(8,128)S(1)} custom-call(f32[8,2,128,256]{3,2,1,0:T(8,128)} %collective-permute-done.low_ref, f32[16,2,128,256]{3,2,1,0:T(8,128)} %all-to-all-done.own_ref, f32[8,2,128,256]{3,2,1,0:T(8,128)S(1)} %collective-permute-done.1.high_ref, f32[16,2,128,256]{3,2,1,0:T(8,128)S(1)} %fusion.table_ref), custom_call_target="tpu_custom_call" | custom-call | flops 67108864 | bytes 16777216 | tf_op jit(solution)/shard_map/pallas_call | solution.py:80
  167.3 2.0 copy-done.1
  169.4 1.4 copy.44
  170.7 1.3 dynamic-slice_add_fusion
  172.1 4.6 %all-to-all-start.1 = ((f32[16,2,128,256]{3,2,1,0:T(8,128)}), f32[16,2,128,256]{3,2,1,0:T(8,128)}, u32[]{:S(2)}, u32[]{:S(2)}) async-start(f32[16,2,128,256]{3,2,1,0:T(8,128)} %copy-done.1), calls=%async_computation.1 | async-start | bytes 8388608 | tf_op jit(solution)/shard_map/all_to_all | solution.py:159
  176.7 0.7 all-reduce.2.cloned.1.call-update
  177.5 53.2 %all-reduce.2.cloned.1.call-done = f32[8,2,64,128]{2,3,1,0:T(8,128)} async-done(((f32[8,2,64,128]{2,3,1,0:T(8,128)}), f32[8,2,64,128]{2,3,1,0:T(8,128)}) %all-reduce.2.cloned.1.call-update) | async-done | bytes 524304 | tf_op jit(solution)/shard_map/psum | solution.py:145
  230.8 1.5 copy.46
  232.8 1.5 collective-permute-start.4
  234.4 6.8 %collective-permute-done.4 = f32[4,2,64,128]{3,2,1,0:T(8,128)S(1)} collective-permute-done((f32[4,2,64,128]{3,2,1,0:T(8,128)S(1)}, f32[4,2,64,128]{3,2,1,0:T(8,128)S(1)}, u32[]{:S(2)}, u32[]{:S(2)}) %collective-permute-start.4) | collective-permute-done | bytes 262176 | tf_op jit(solution)/shard_map/ppermute | solution.py:154
  241.2 0.8 maximum_bitcast_fusion
  242.0 4.7 %copy.45 = f32[2,4,2,2,128,256]{5,4,3,2,1,0:T(8,128)} copy(f32[2,4,2,2,128,256]{5,4,2,0,1,3:T(8,128)} %bitcast.15) | data formatting | bytes 8388608 | tf_op jit(solution)/shard_map/transpose | solution.py:160
  (29 shorter events, 1.7 us)
Async XLA Ops:
  7.2 132.8 %copy-start = (f32[256,128]{1,0:T(8,128)S(1)}, f32[256,128]{1,0:T(8,128)}, u32[]{:S(2)}) copy-start(f32[256,128]{1,0:T(8,128)} %param.7) | copy-start | bytes 393220
  11.9 6.1 %copy-start.3 = (f32[32]{0:T(128)S(1)}, f32[32]{0:T(128)}, u32[]{:S(2)}) copy-start(f32[32]{0:T(128)} %param.8) | copy-start | bytes 388
  11.9 6.2 %copy-start.2 = (s32[32]{0:T(128)S(1)}, s32[32]{0:T(128)}, u32[]{:S(2)}) copy-start(s32[32]{0:T(128)} %param.9) | copy-start | bytes 388
  11.9 63.6 %all-to-all-start = ((f32[16,2,128,256]{3,2,1,0:T(8,128)}), f32[16,2,128,256]{3,2,1,0:T(8,128)}, u32[]{:S(2)}, u32[]{:S(2)}) async-start(f32[16,2,128,256]{3,2,1,0:T(8,128)} %bitcast.50), calls=%async_computation | async-start | bytes 8388608 | tf_op jit(solution)/shard_map/all_to_all | solution.py:112
  17.2 50.8 %all-gather.2.cloned.1.call-start = ((), (), s32[]{:S(2)}) async-start(), calls=%async_computation.2 | async-start | bytes 2621440 | tf_op jit(solution)/shard_map/all_gather | solution.py:106
  80.1 49.5 %collective-permute-start.1 = (f32[8,2,128,256]{3,2,1,0:T(8,128)}, f32[8,2,128,256]{3,2,1,0:T(8,128)S(1)}, u32[]{:S(2)}, u32[]{:S(2)}) collective-permute-start(f32[8,2,128,256]{3,2,1,0:T(8,128)} %get-tuple-element.18), channel_id=1, source_target_pairs={{8,0},{12,4},{16,8},{20,12},{24,16},{28,20},{9,1},{13,5},{17,9},{2... | collective-permute-start | bytes 6291464 | tf_op jit(solution)/shard_map/ppermute | solution.py:127
  81.4 60.3 %collective-permute-start = (f32[8,2,128,256]{3,2,1,0:T(8,128)}, f32[8,2,128,256]{3,2,1,0:T(8,128)}, u32[]{:S(2)}, u32[]{:S(2)}) collective-permute-start(f32[8,2,128,256]{3,2,1,0:T(8,128)} %get-tuple-element.19), channel_id=1, source_target_pairs={{0,8},{4,12},{8,16},{12,20},{16,24},{20,28},{1,9},{5,13},{9,17},{1... | collective-permute-start | bytes 6291464 | tf_op jit(solution)/shard_map/ppermute | solution.py:128
  87.3 59.6 %collective-permute-start.2 = (f32[16,2,128,128]{3,0,2,1:T(8,128)}, f32[16,2,128,128]{3,0,2,1:T(8,128)}, u32[]{:S(2)}, u32[]{:S(2)}) collective-permute-start(f32[16,2,128,128]{3,0,2,1:T(8,128)} %fusion.4), channel_id=1, source_target_pairs={{0,4},{4,0},{8,12},{12,8},{16,20},{20,16},{24,28},{28,24},{1,5},{5... | collective-permute-start | bytes 6291464 | tf_op jit(solution)/shard_map/ppermute | solution.py:130
  145.4 23.9 %collective-permute-start.3 = (f32[8,2,64,128]{3,2,1,0:T(8,128)}, f32[8,2,64,128]{3,2,1,0:T(8,128)}, u32[]{:S(2)}, u32[]{:S(2)}) collective-permute-start(f32[8,2,64,128]{3,2,1,0:T(8,128)} %copy.43), channel_id=1, source_target_pairs={{0,4},{4,0},{8,12},{12,8},{16,20},{20,16},{24,28},{28,24},{1,5},{5... | collective-permute-start | bytes 1572872 | tf_op jit(solution)/shard_map/ppermute | solution.py:142
  167.3 2.0 copy-start.1
  172.1 70.0 %all-to-all-start.1 = ((f32[16,2,128,256]{3,2,1,0:T(8,128)}), f32[16,2,128,256]{3,2,1,0:T(8,128)}, u32[]{:S(2)}, u32[]{:S(2)}) async-start(f32[16,2,128,256]{3,2,1,0:T(8,128)} %copy-done.1), calls=%async_computation.1 | async-start | bytes 8388608 | tf_op jit(solution)/shard_map/all_to_all | solution.py:159
  176.6 54.1 %all-reduce.2.cloned.1.call-start = ((), (), s32[]{:S(2)}) async-start(), calls=%async_computation.3 | async-start | bytes 2097152 | tf_op jit(solution)/shard_map/psum | solution.py:145
  232.8 8.3 %collective-permute-start.4 = (f32[4,2,64,128]{3,2,1,0:T(8,128)S(1)}, f32[4,2,64,128]{3,2,1,0:T(8,128)S(1)}, u32[]{:S(2)}, u32[]{:S(2)}) collective-permute-start(f32[4,2,64,128]{3,2,1,0:T(8,128)S(1)} %get-tuple-element.17), channel_id=1, source_target_pairs={{0,4},{4,0},{8,12},{12,8},{16,20},{20,16},{24,28},{28,24},{1,5},{5... | collective-permute-start | bytes 786440 | tf_op jit(solution)/shard_map/ppermute | solution.py:154
Sparse Core Ops, SparseCore 0:
  19.6 48.3 all-gather.1
  179.8 50.8 all-reduce.1

commit v3 on v2

--- a/solution.py
+++ b/solution.py
@@ -11,6 +11,7 @@
 TILE = 8
 LANES = 128
 BLOCK = 4
+CHUNKS = 2
 
 
 def cell_of(low_ref, own_ref, high_ref):
@@ -107,14 +108,25 @@
     own_w = phonon.shape[0]
     total_w = own_w * n_energy
 
-    pieces = green.reshape(own, slabs, 2, halves, rows, size).transpose(3, 1, 0, 2, 4, 5)
-    pieces = pieces.reshape(team * own, 2, rows, size)
-    mine = lax.all_to_all(pieces, both, 0, 0, axis_index_groups=groups, tiled=True)
-
+    chunks = CHUNKS if rows % (CHUNKS * TILE) == 0 else 1
+    depth = rows // chunks
+    pieces = green.reshape(own, slabs, 2, halves, chunks, depth, size)
     up = [(i, i + halves) for i in range(n_energy - halves)]
     down = [(i + halves, i) for i in range(n_energy - halves)]
-
-    my_coupling = lax.dynamic_slice_in_dim(coupling, column * rows, rows, 0)
+    mine, high, low = [], [], []
+    for c in range(chunks):
+        piece = pieces[:, :, :, :, c].transpose(3, 1, 0, 2, 4, 5).reshape(team * own, 2, depth, size)
+        if c > 0:
+            piece, mine[-1] = lax.optimization_barrier((piece, mine[-1]))
+        mine.append(lax.all_to_all(piece, both, 0, 0, axis_index_groups=groups, tiled=True))
+    mine[-1], every = lax.optimization_barrier((mine[-1], every))
+    for c in range(chunks):
+        high.append(lax.ppermute(mine[c][:levels], "energy", down))
+        low.append(lax.ppermute(mine[c][-levels:], "energy", up))
+    high[-1], low = lax.optimization_barrier((high[-1], low))
+    my_coupling = [
+        lax.dynamic_slice_in_dim(coupling, column * rows + c * depth, depth, 0) for c in range(chunks)
+    ]
 
     steps = jnp.arange(1, levels + 1, dtype=jnp.int32)
     select = (shifts[None, :] == steps[:, None]).astype(jnp.float32) / math.sqrt(total_w)
@@ -123,25 +135,27 @@
     weights = lax.dynamic_index_in_dim(weights, column, 2, keepdims=False).reshape(2 * levels, -1)
     mixed = jnp.dot(weights, every.reshape(turns * own_w, -1), precision=lax.Precision.HIGHEST)
     mixed = mixed.reshape(2 * levels, 2, *every.shape[3:])
-    mine, mixed = lax.optimization_barrier((mine, mixed))
-    high = lax.ppermute(mine[:levels], "energy", down)
-    low = lax.ppermute(mine[-levels:], "energy", up)
     if halves == 2:
         mixed = mixed + lax.ppermute(mixed, "energy", swap)
-    half = jnp.einsum("im,lpmk->lpik", my_coupling, mixed, precision=lax.Precision.HIGH)
-    tables = jnp.einsum("lpik,jk->lpij", half, coupling, precision=lax.Precision.HIGH)
-
-    pairs = tiled(functools.partial(pairs_kernel, 1.0 / math.sqrt(total_e)), levels, mine, high)
-    right = jnp.einsum("lpbc,cj->lpbj", pairs, coupling, precision=lax.Precision.HIGH)
-    part = jnp.einsum("bi,lpbj->lpij", my_coupling, right, precision=lax.Precision.HIGH)
-    low, part = lax.optimization_barrier((low, part))
+    part = 0.0
+    for c in range(chunks):
+        pairs = tiled(functools.partial(pairs_kernel, 1.0 / math.sqrt(total_e)), levels, mine[c], high[c])
+        right = jnp.einsum("lpbc,cj->lpbj", pairs, coupling, precision=lax.Precision.HIGH)
+        part = part + jnp.einsum("bi,lpbj->lpij", my_coupling[c], right, precision=lax.Precision.HIGH)
     modes = part.shape[2] // halves
     kept = lax.dynamic_slice_in_dim(part, column * modes, modes, 2)
     if halves == 2:
         sent = lax.dynamic_slice_in_dim(part, (1 - column) * modes, modes, 2)
         kept = kept + lax.ppermute(sent, "energy", swap)
-    sigma_mine = tiled(sigma_kernel, team * own, low, mine, high, tables)
-    sigma_mine, kept = lax.optimization_barrier((sigma_mine, kept))
+    back = []
+    for c in range(chunks):
+        half = jnp.einsum("im,lpmk->lpik", my_coupling[c], mixed, precision=lax.Precision.HIGH)
+        table = jnp.einsum("lpik,jk->lpij", half, coupling, precision=lax.Precision.HIGH)
+        sigma_mine = tiled(sigma_kernel, team * own, low[c], mine[c], high[c], table)
+        if c == 0:
+            sigma_mine, kept = lax.optimization_barrier((sigma_mine, kept))
+        got = lax.all_to_all(sigma_mine, both, 0, 0, axis_index_groups=groups, tiled=True)
+        back.append(got.reshape(halves, slabs, own, 2, depth, size))
     total = lax.psum(kept, "energy", axis_index_groups=lines)
 
     def chosen(holder):
@@ -156,9 +170,8 @@
         polar = jnp.concatenate([first, second], axis=2)
     polar = polar[:, None]
 
-    back = lax.all_to_all(sigma_mine, both, 0, 0, axis_index_groups=groups, tiled=True)
-    back = back.reshape(halves, slabs, own, 2, rows, size).transpose(2, 1, 3, 0, 4, 5)
-    return (back.reshape(green.shape), polar)
+    sigma = jnp.stack([g.transpose(2, 1, 3, 0, 4, 5) for g in back], axis=4)
+    return (sigma.reshape(green.shape), polar)
 
 
 def solution(mesh):

time: 255 us -> 264 us (1.035)
  starting transfers between devices: 21.6 us -> 36.9 us
  local copies, waits for them, and re-layouts: 26.2 us -> 21.2 us
  waiting for transfers between devices: 152 us -> 148 us
  other arithmetic: 5.47 us -> 9.19 us
    all_gather x1, waiting for transfers between devices: 49.6 us -> 15.5 us  [shards(): lax.all_gather(phonon, 'energy', axis=0, axis_index_groups=lines, tiled=T...]
    ppermute x1, waiting for transfers between devices: 0.01 us -> 27.5 us  [shards(): kept = kept + lax.ppermute(sent, 'energy', swap)]
    ppermute x2 -> x4, waiting for transfers between devices: 40.8 us -> 15.4 us  [the longest x2 13.5 us: shards(): low.append(lax.ppermute(mine[c][-levels:], 'energy', up))]
    all_to_all x1 -> x2, waiting for transfers between devices: 0.01 us -> 23.1 us  [shards(): lax.all_to_all(piece, both, 0, 0, axis_index_groups=groups, tiled=True)]
    all_to_all x1 -> x2, waiting for transfers between devices: 0.01 us -> 15.1 us  [shards(): lax.all_to_all(sigma_mine, both, 0, 0, axis_index_groups=groups, tiled=True)]
    psum x1, waiting for transfers between devices: 53.2 us -> 44.2 us  [shards(): total = lax.psum(kept, 'energy', axis_index_groups=lines)]
    ppermute x2 -> x4, starting transfers between devices: 7.19 us -> 14.7 us  [the longest x2 12.2 us: shards(): low.append(lax.ppermute(mine[c][-levels:], 'energy', up))]
    reshape x1 -> x0, local copies, waits for them, and re-layouts: 4.69 us -> none  [shards(): green.reshape(own, slabs, 2, halves, rows, size).transpose(3, 1, 0, 2, 4, 5)]
  transfers between devices with their start and end apart: 9 -> 13, of which waited for: 4 -> 9; matrix products, arithmetic and copies ran while one was open for 9% -> 9% of each run, Pallas kernels for 9% -> 6%
where the time goes in v3:
time: 264 us; the launch traced here: 263 us
  waiting for transfers between devices  148 us (56%)
  starting transfers between devices  36.9 us (14%)
  Pallas kernels  23 us (9%)
  local copies, waits for them, and re-layouts  21.2 us (8%)
  between operations  14.3 us (5%)
  matrix products  11 us (4%)
  other arithmetic  9.19 us (3%)
    psum x1, waiting for transfers between devices, shards(): total = lax.psum(kept, 'energy', axis_index_groups=lines)  44.2 us
    ppermute x1, waiting for transfers between devices, shards(): kept = kept + lax.ppermute(sent, 'energy', swap)  27.5 us
    all_to_all x2, waiting for transfers between devices, shards(): lax.all_to_all(piece, both, 0, 0, axis_index_groups=groups, tiled=True)  23.1 us
    pallas_call x4, Pallas kernels, tiled(): pl.pallas_call(body, grid=(rows // TILE,), in_specs=[spec(a.shape[0]) for...  23 us
    all_gather x1, waiting for transfers between devices, shards(): lax.all_gather(phonon, 'energy', axis=0, axis_index_groups=lines, tiled=T...  15.5 us
    all_to_all x2, waiting for transfers between devices, shards(): lax.all_to_all(sigma_mine, both, 0, 0, axis_index_groups=groups, tiled=True)  15.1 us
    ppermute x2, waiting for transfers between devices, shards(): low.append(lax.ppermute(mine[c][-levels:], 'energy', up))  13.5 us
    ppermute x2, starting transfers between devices, shards(): low.append(lax.ppermute(mine[c][-levels:], 'energy', up))  12.2 us
  transfers between devices with their start and end apart: 13, of which 9 were waited for; matrix products, arithmetic and copies ran while one was open for 9% of the time, Pallas kernels for 6%

profile of v3, /device:TPU:0, one launch (start us, length us, event | category | flops | bytes accessed | tf_op | source)
XLA Modules:
  0.0 263.4 jit_solution(15340296952952986525)
XLA Ops:
  7.2 4.1 %fusion.35 = (f32[2,4,2,2,1,64,256]{6,5,4,3,2,1,0:T(8,128)S(1)}, f32[2,4,2,2,1,64,256]{6,5,4,3,2,1,0:T(8,128)}) fusion(f32[2,4,2,2,2,64,256]{6,5,4,3,2,1,0:T(8,128)} %bitcast.86), kind=kLoop, calls=%fused_computation.49 | loop fusion | bytes 8388608 | tf_op jit(solution)/shard_map/slice | solution.py:118
  11.3 1.6 copy.48
  12.8 5.2 %all-to-all-start = ((f32[16,2,64,256]{3,2,1,0:T(8,128)}), f32[16,2,64,256]{3,2,1,0:T(8,128)S(1)}, u32[]{:S(2)}, u32[]{:S(2)}) async-start(f32[16,2,64,256]{3,2,1,0:T(8,128)} %bitcast.83), calls=%async_computation | async-start | bytes 4194304 | tf_op jit(solution)/shard_map/all_to_all | solution.py:121
  18.7 3.2 %copy.47 = f32[2,4,2,2,1,64,256]{6,5,2,0,1,3,4:T(8,128)} copy(f32[2,4,2,2,1,64,256]{6,5,4,3,2,1,0:T(8,128)} %get-tuple-element.25) | data formatting | bytes 4194304
  21.9 21.8 %all-to-all-done.own_ref = f32[16,2,64,256]{3,2,1,0:T(8,128)S(1)} async-done(((f32[16,2,64,256]{3,2,1,0:T(8,128)}), f32[16,2,64,256]{3,2,1,0:T(8,128)S(1)}, u32[]{:S(2)}, u32[]{:S(2)}) %all-to-all-start) | async-done | bytes 2097184 | tf_op jit(solution)/shard_map/all_to_all | solution.py:121
  43.7 4.5 %all-to-all-start.1 = ((f32[16,2,64,256]{3,2,1,0:T(8,128)}), f32[16,2,64,256]{3,2,1,0:T(8,128)}, u32[]{:S(2)}, u32[]{:S(2)}) async-start(f32[16,2,64,256]{3,2,1,0:T(8,128)} %bitcast.82), calls=%async_computation.1 | async-start | bytes 4194304 | tf_op jit(solution)/shard_map/all_to_all | solution.py:121
  48.5 1.6 fusion.36
  51.5 5.6 %collective-permute-start.1 = (f32[8,2,64,256]{3,2,1,0:T(8,128)}, f32[8,2,64,256]{3,2,1,0:T(8,128)}, u32[]{:S(2)}, u32[]{:S(2)}) collective-permute-start(f32[8,2,64,256]{3,2,1,0:T(8,128)} %get-tuple-element.27), channel_id=1, source_target_pairs={{0,8},{4,12},{8,16},{12,20},{16,24},{20,28},{1,9},{5,13},{9,17},{1... | collective-permute-start | bytes 3145736 | tf_op jit(solution)/shard_map/ppermute | solution.py:125
  57.1 15.5 %all-gather.2.cloned.1.call-done = f32[16,1,2,128,128]{4,3,2,1,0:T(8,128)} async-done(((f32[4,1,2,128,128]{4,3,2,1,0:T(8,128)}), f32[16,1,2,128,128]{4,3,2,1,0:T(8,128)}) %all-gather.2.cloned.1.call-update) | async-done | bytes 2097168 | tf_op jit(solution)/shard_map/all_gather | solution.py:107
  73.9 3.3 %fusion.37 = (f32[8,2,64,256]{3,2,1,0:T(8,128)}, f32[8,2,64,256]{3,2,1,0:T(8,128)}) fusion(f32[16,2,64,256]{3,2,1,0:T(8,128)} %all-to-all-done.1.own_ref), kind=kLoop, calls=%fused_computation.51 | loop fusion | bytes 4194304 | tf_op jit(solution)/shard_map/slice | solution.py:125
  77.2 6.6 %collective-permute-start.2 = (f32[8,2,64,256]{3,2,1,0:T(8,128)}, f32[8,2,64,256]{3,2,1,0:T(8,128)}, u32[]{:S(2)}, u32[]{:S(2)}) collective-permute-start(f32[8,2,64,256]{3,2,1,0:T(8,128)} %get-tuple-element.28), channel_id=1, source_target_pairs={{0,8},{4,12},{8,16},{12,20},{16,24},{20,28},{1,9},{5,13},{9,17},{1... | collective-permute-start | bytes 3145736 | tf_op jit(solution)/shard_map/ppermute | solution.py:125
  86.7 4.2 %fusion = f32[16,2,128,128]{3,0,2,1:T(8,128)} fusion(f32[16,16,1,1]{0,1,3,2:T(8,128)S(1)} %bitcast.89, f32[2,128,128,16]{2,1,0,3:T(8,128)S(1)} %bitcast.84), kind=kOutput, calls=%fused_computation.2 | convolution fusion | flops 100663296 | bytes 4195328 | tf_op jit(solution)/shard_map/dot_general | solution.py:136
  92.1 2.6 %shard_map.69 = f32[8,2,64,256]{3,2,1,0:T(8,128)S(1)} custom-call(f32[16,2,64,256]{3,2,1,0:T(8,128)S(1)} %all-to-all-done.own_ref, f32[8,2,64,256]{3,2,1,0:T(8,128)S(1)} %collective-permute-done.3.high_ref), custom_call_target="tpu_custom_call" | custom-call | flops 16777216 | bytes 4194304 | tf_op jit(solution)/shard_map/pallas_call | solution.py:81
  96.0 13.5 %collective-permute-done.2.low_ref = f32[8,2,64,256]{3,2,1,0:T(8,128)} collective-permute-done((f32[8,2,64,256]{3,2,1,0:T(8,128)}, f32[8,2,64,256]{3,2,1,0:T(8,128)}, u32[]{:S(2)}, u32[]{:S(2)}) %collective-permute-start.2) | collective-permute-done | bytes 1048608 | tf_op jit(solution)/shard_map/ppermute | solution.py:125
  109.5 1.8 collective-permute-done.high_ref
  111.3 5.5 %shard_map.70 = f32[8,2,64,256]{3,2,1,0:T(8,128)S(1)} custom-call(f32[16,2,64,256]{3,2,1,0:T(8,128)} %all-to-all-done.1.own_ref, f32[8,2,64,256]{3,2,1,0:T(8,128)} %collective-permute-done.high_ref), custom_call_target="tpu_custom_call" | custom-call | flops 16777216 | bytes 4194304 | tf_op jit(solution)/shard_map/pallas_call | solution.py:81
  119.9 1.5 collective-permute-start.5
  121.4 27.5 %collective-permute-done.5 = f32[8,2,64,128]{3,2,1,0:T(8,128)} collective-permute-done((f32[8,2,64,128]{3,2,1,0:T(8,128)}, f32[8,2,64,128]{3,2,1,0:T(8,128)}, u32[]{:S(2)}, u32[]{:S(2)}) %collective-permute-start.5) | collective-permute-done | bytes 524320 | tf_op jit(solution)/shard_map/ppermute | solution.py:149
  148.9 2.1 bitcast_add_fusion
  151.0 2.5 add.67
  155.8 6.6 %shard_map.68 = f32[16,2,64,256]{3,2,1,0:T(8,128)S(1)} custom-call(f32[8,2,64,256]{3,2,1,0:T(8,128)} %collective-permute-done.1.low_ref, f32[16,2,64,256]{3,2,1,0:T(8,128)S(1)} %all-to-all-done.own_ref, f32[8,2,64,256]{3,2,1,0:T(8,128)S(1)} %collective-permute-done.3.high_ref, f32[16,2,64,256]{3,2,1,0:T(8,128)S(1)} %fusion.18.table_ref), custom_call_target="tpu_custom_call" | custom-call | flops 33554432 | bytes 8388608 | tf_op jit(solution)/shard_map/pallas_call | solution.py:81
  162.4 1.3 copy-done.1
  163.8 4.7 %all-to-all-start.2 = ((f32[16,2,64,256]{3,2,1,0:T(8,128)}), f32[16,2,64,256]{3,2,1,0:T(8,128)}, u32[]{:S(2)}, u32[]{:S(2)}) async-start(f32[16,2,64,256]{3,2,1,0:T(8,128)} %copy-done.1), calls=%async_computation.2 | async-start | bytes 4194304 | tf_op jit(solution)/shard_map/all_to_all | solution.py:157
  170.7 8.2 %shard_map.71 = f32[16,2,64,256]{3,2,1,0:T(8,128)} custom-call(f32[8,2,64,256]{3,2,1,0:T(8,128)} %collective-permute-done.2.low_ref, f32[16,2,64,256]{3,2,1,0:T(8,128)} %all-to-all-done.1.own_ref, f32[8,2,64,256]{3,2,1,0:T(8,128)} %collective-permute-done.high_ref, f32[16,2,64,256]{3,2,1,0:T(8,128)S(1)} %fusion.12.table_ref), custom_call_target="tpu_custom_call" | custom-call | flops 33554432 | bytes 8388608 | tf_op jit(solution)/shard_map/pallas_call | solution.py:81
  178.9 15.1 %all-to-all-done.2 = f32[16,2,64,256]{3,2,1,0:T(8,128)} async-done(((f32[16,2,64,256]{3,2,1,0:T(8,128)}), f32[16,2,64,256]{3,2,1,0:T(8,128)}, u32[]{:S(2)}, u32[]{:S(2)}) %all-to-all-start.2) | async-done | bytes 2097184 | tf_op jit(solution)/shard_map/all_to_all | solution.py:157
  194.0 3.6 %all-to-all-start.3 = ((f32[16,2,64,256]{3,2,1,0:T(8,128)}), f32[16,2,64,256]{3,2,1,0:T(8,128)S(1)}, u32[]{:S(2)}, u32[]{:S(2)}) async-start(f32[16,2,64,256]{3,2,1,0:T(8,128)} %shard_map.71), calls=%async_computation.3 | async-start | bytes 4194304 | tf_op jit(solution)/shard_map/all_to_all | solution.py:157
  198.5 44.2 %all-reduce.2.cloned.1.call-done = f32[8,2,64,128]{3,2,1,0:T(8,128)} async-done(((f32[8,2,64,128]{3,2,1,0:T(8,128)}), f32[8,2,64,128]{3,2,1,0:T(8,128)}) %all-reduce.2.cloned.1.call-update) | async-done | bytes 524304 | tf_op jit(solution)/shard_map/psum | solution.py:159
  242.7 1.6 select_reduce_fusion.1
  244.3 1.5 collective-permute-start.6
  245.9 5.6 %collective-permute-done.6 = f32[4,2,64,128]{3,2,1,0:T(8,128)S(1)} collective-permute-done((f32[4,2,64,128]{3,2,1,0:T(8,128)S(1)}, f32[4,2,64,128]{3,2,1,0:T(8,128)S(1)}, u32[]{:S(2)}, u32[]{:S(2)}) %collective-permute-start.6) | collective-permute-done | bytes 262176 | tf_op jit(solution)/shard_map/ppermute | solution.py:168
  252.4 1.9 pad_maximum_fusion
  254.3 2.3 copy.40
  (52 shorter events, 18.4 us)
Async XLA Ops:
  7.2 87.6 %copy-start = (f32[256,128]{1,0:T(8,128)S(1)}, f32[256,128]{1,0:T(8,128)}, u32[]{:S(2)}) copy-start(f32[256,128]{1,0:T(8,128)} %param.7) | copy-start | bytes 393220
  12.8 30.9 %all-to-all-start = ((f32[16,2,64,256]{3,2,1,0:T(8,128)}), f32[16,2,64,256]{3,2,1,0:T(8,128)S(1)}, u32[]{:S(2)}, u32[]{:S(2)}) async-start(f32[16,2,64,256]{3,2,1,0:T(8,128)} %bitcast.83), calls=%async_computation | async-start | bytes 4194304 | tf_op jit(solution)/shard_map/all_to_all | solution.py:121
  18.0 54.6 %all-gather.2.cloned.1.call-start = ((), (), s32[]{:S(2)}) async-start(), calls=%async_computation.4 | async-start | bytes 2621440 | tf_op jit(solution)/shard_map/all_gather | solution.py:107
  43.7 4.5 %copy-start.7 = (f32[32]{0:T(128)S(1)}, f32[32]{0:T(128)}, u32[]{:S(2)}) copy-start(f32[32]{0:T(128)} %param.8) | copy-start | bytes 388
  43.7 4.7 %copy-start.6 = (s32[32]{0:T(128)S(1)}, s32[32]{0:T(128)}, u32[]{:S(2)}) copy-start(s32[32]{0:T(128)} %param.9) | copy-start | bytes 388
  43.7 30.2 %all-to-all-start.1 = ((f32[16,2,64,256]{3,2,1,0:T(8,128)}), f32[16,2,64,256]{3,2,1,0:T(8,128)}, u32[]{:S(2)}, u32[]{:S(2)}) async-start(f32[16,2,64,256]{3,2,1,0:T(8,128)} %bitcast.82), calls=%async_computation.1 | async-start | bytes 4194304 | tf_op jit(solution)/shard_map/all_to_all | solution.py:121
  50.1 42.0 %collective-permute-start.3 = (f32[8,2,64,256]{3,2,1,0:T(8,128)}, f32[8,2,64,256]{3,2,1,0:T(8,128)S(1)}, u32[]{:S(2)}, u32[]{:S(2)}) collective-permute-start(f32[8,2,64,256]{3,2,1,0:T(8,128)} %get-tuple-element.26), channel_id=1, source_target_pairs={{8,0},{12,4},{16,8},{20,12},{24,16},{28,20},{9,1},{13,5},{17,9},{2... | collective-permute-start | bytes 3145736 | tf_op jit(solution)/shard_map/ppermute | solution.py:124
  51.5 44.5 %collective-permute-start.1 = (f32[8,2,64,256]{3,2,1,0:T(8,128)}, f32[8,2,64,256]{3,2,1,0:T(8,128)}, u32[]{:S(2)}, u32[]{:S(2)}) collective-permute-start(f32[8,2,64,256]{3,2,1,0:T(8,128)} %get-tuple-element.27), channel_id=1, source_target_pairs={{0,8},{4,12},{8,16},{12,20},{16,24},{20,28},{1,9},{5,13},{9,17},{1... | collective-permute-start | bytes 3145736 | tf_op jit(solution)/shard_map/ppermute | solution.py:125
  73.9 11.2 %copy-start.5 = (f32[16,1,2,128,128]{4,3,2,1,0:T(8,128)S(1)}, f32[16,1,2,128,128]{4,3,2,1,0:T(8,128)}, u32[]{:S(2)}) copy-start(f32[16,1,2,128,128]{4,3,2,1,0:T(8,128)} %all-gather.2.cloned.1.call-done) | copy-start | bytes 6291460
  77.2 32.3 %collective-permute-start.2 = (f32[8,2,64,256]{3,2,1,0:T(8,128)}, f32[8,2,64,256]{3,2,1,0:T(8,128)}, u32[]{:S(2)}, u32[]{:S(2)}) collective-permute-start(f32[8,2,64,256]{3,2,1,0:T(8,128)} %get-tuple-element.28), channel_id=1, source_target_pairs={{0,8},{4,12},{8,16},{12,20},{16,24},{20,28},{1,9},{5,13},{9,17},{1... | collective-permute-start | bytes 3145736 | tf_op jit(solution)/shard_map/ppermute | solution.py:125
  83.7 27.6 %collective-permute-start = (f32[8,2,64,256]{3,2,1,0:T(8,128)}, f32[8,2,64,256]{3,2,1,0:T(8,128)}, u32[]{:S(2)}, u32[]{:S(2)}) collective-permute-start(f32[8,2,64,256]{3,2,1,0:T(8,128)} %get-tuple-element.29), channel_id=1, source_target_pairs={{8,0},{12,4},{16,8},{20,12},{24,16},{28,20},{9,1},{13,5},{17,9},{2... | collective-permute-start | bytes 3145736 | tf_op jit(solution)/shard_map/ppermute | solution.py:124
  90.9 60.0 %collective-permute-start.4 = (f32[16,2,128,128]{3,0,2,1:T(8,128)}, f32[16,2,128,128]{3,0,2,1:T(8,128)}, u32[]{:S(2)}, u32[]{:S(2)}) collective-permute-start(f32[16,2,128,128]{3,0,2,1:T(8,128)} %fusion), channel_id=1, source_target_pairs={{0,4},{4,0},{8,12},{12,8},{16,20},{20,16},{24,28},{28,24},{1,5},{5... | collective-permute-start | bytes 6291464 | tf_op jit(solution)/shard_map/ppermute | solution.py:139
  118.0 1.0 copy-start.4
  119.9 29.0 %collective-permute-start.5 = (f32[8,2,64,128]{3,2,1,0:T(8,128)}, f32[8,2,64,128]{3,2,1,0:T(8,128)}, u32[]{:S(2)}, u32[]{:S(2)}) collective-permute-start(f32[8,2,64,128]{3,2,1,0:T(8,128)} %dynamic-slice_bitcast_fusion), channel_id=1, source_target_pairs={{0,4},{4,0},{8,12},{12,8},{16,20},{20,16},{24,28},{28,24},{1,5},{5... | collective-permute-start | bytes 1572872 | tf_op jit(solution)/shard_map/ppermute | solution.py:149
  153.5 1.3 copy-start.2
  162.4 1.4 copy-start.1
  163.8 4.7 %copy-start.3 = (f32[16,2,128,128]{3,0,2,1:T(8,128)S(1)}, f32[16,2,128,128]{3,0,2,1:T(8,128)}, u32[]{:S(2)}) copy-start(f32[16,2,128,128]{3,0,2,1:T(8,128)} %copy-done.2) | copy-start | bytes 6291460
  163.8 30.2 %all-to-all-start.2 = ((f32[16,2,64,256]{3,2,1,0:T(8,128)}), f32[16,2,64,256]{3,2,1,0:T(8,128)}, u32[]{:S(2)}, u32[]{:S(2)}) async-start(f32[16,2,64,256]{3,2,1,0:T(8,128)} %copy-done.1), calls=%async_computation.2 | async-start | bytes 4194304 | tf_op jit(solution)/shard_map/all_to_all | solution.py:157
  194.0 58.4 %all-to-all-start.3 = ((f32[16,2,64,256]{3,2,1,0:T(8,128)}), f32[16,2,64,256]{3,2,1,0:T(8,128)S(1)}, u32[]{:S(2)}, u32[]{:S(2)}) async-start(f32[16,2,64,256]{3,2,1,0:T(8,128)} %shard_map.71), calls=%async_computation.3 | async-start | bytes 4194304 | tf_op jit(solution)/shard_map/all_to_all | solution.py:157
  197.6 45.1 %all-reduce.2.cloned.1.call-start = ((), (), s32[]{:S(2)}) async-start(), calls=%async_computation.5 | async-start | bytes 1048576 | tf_op jit(solution)/shard_map/psum | solution.py:159
  244.3 7.1 %collective-permute-start.6 = (f32[4,2,64,128]{3,2,1,0:T(8,128)S(1)}, f32[4,2,64,128]{3,2,1,0:T(8,128)S(1)}, u32[]{:S(2)}, u32[]{:S(2)}) collective-permute-start(f32[4,2,64,128]{3,2,1,0:T(8,128)S(1)} %get-tuple-element.23), channel_id=1, source_target_pairs={{0,4},{4,0},{8,12},{12,8},{16,20},{20,16},{24,28},{28,24},{1,5},{5... | collective-permute-start | bytes 786440 | tf_op jit(solution)/shard_map/ppermute | solution.py:168
Sparse Core Ops, SparseCore 0:
  20.4 52.1 all-gather.1
  201.3 41.3 all-reduce.1

commit v4 on v3

--- a/solution.py
+++ b/solution.py
@@ -142,21 +142,18 @@
         pairs = tiled(functools.partial(pairs_kernel, 1.0 / math.sqrt(total_e)), levels, mine[c], high[c])
         right = jnp.einsum("lpbc,cj->lpbj", pairs, coupling, precision=lax.Precision.HIGH)
         part = part + jnp.einsum("bi,lpbj->lpij", my_coupling[c], right, precision=lax.Precision.HIGH)
-    modes = part.shape[2] // halves
-    kept = lax.dynamic_slice_in_dim(part, column * modes, modes, 2)
-    if halves == 2:
-        sent = lax.dynamic_slice_in_dim(part, (1 - column) * modes, modes, 2)
-        kept = kept + lax.ppermute(sent, "energy", swap)
+    mixed, part = lax.optimization_barrier((mixed, part))
+    total = lax.psum(part, "energy", axis_index_groups=lines)
+
     back = []
     for c in range(chunks):
         half = jnp.einsum("im,lpmk->lpik", my_coupling[c], mixed, precision=lax.Precision.HIGH)
         table = jnp.einsum("lpik,jk->lpij", half, coupling, precision=lax.Precision.HIGH)
         sigma_mine = tiled(sigma_kernel, team * own, low[c], mine[c], high[c], table)
         if c == 0:
-            sigma_mine, kept = lax.optimization_barrier((sigma_mine, kept))
+            sigma_mine, total = lax.optimization_barrier((sigma_mine, total))
         got = lax.all_to_all(sigma_mine, both, 0, 0, axis_index_groups=groups, tiled=True)
         back.append(got.reshape(halves, slabs, own, 2, depth, size))
-    total = lax.psum(kept, "energy", axis_index_groups=lines)
 
     def chosen(holder):
         own_shifts = lax.dynamic_slice_in_dim(shifts, holder * own_w, own_w, 0)
@@ -165,9 +162,7 @@
 
     polar = chosen(lax.axis_index("energy"))
     if halves == 2:
-        other = lax.ppermute(chosen(lax.axis_index("energy") + 1 - 2 * column), "energy", swap)
-        first, second = jnp.where(column == 0, polar, other), jnp.where(column == 0, other, polar)
-        polar = jnp.concatenate([first, second], axis=2)
+        polar = polar + lax.ppermute(chosen(lax.axis_index("energy") + 1 - 2 * column), "energy", swap)
     polar = polar[:, None]
 
     sigma = jnp.stack([g.transpose(2, 1, 3, 0, 4, 5) for g in back], axis=4)

time: 264 us -> 270 us (1.023)
  waiting for transfers between devices: 148 us -> 153 us
  matrix products: 11 us -> 14.3 us
    ppermute x1 -> x0, waiting for transfers between devices: 27.5 us -> none  [shards(): kept = kept + lax.ppermute(sent, 'energy', swap)]
    ppermute x1, waiting for transfers between devices: 5.61 us -> 32.1 us  [shards(): lax.ppermute(chosen(lax.axis_index('energy') + 1 - 2 * column), 'energy',...]
    ppermute x2, waiting for transfers between devices: 13.5 us -> 29.4 us  [shards(): low.append(lax.ppermute(mine[c][-levels:], 'energy', up))]
    all_to_all x2, waiting for transfers between devices: 15.1 us -> 0.01 us  [shards(): lax.all_to_all(sigma_mine, both, 0, 0, axis_index_groups=groups, tiled=True)]
    all_gather x1, waiting for transfers between devices: 15.5 us -> 20.8 us  [shards(): lax.all_gather(phonon, 'energy', axis=0, axis_index_groups=lines, tiled=T...]
    unnamed x20 -> x16, local copies, waits for them, and re-layouts: 8.83 us -> 10.6 us
  transfers between devices with their start and end apart: 13 -> 12, of which waited for: 9 -> 7; matrix products, arithmetic and copies ran while one was open for 9% -> 10% of each run, Pallas kernels for 6% -> 6%
where the time goes in v4:
time: 270 us; the launch traced here: 269 us
  waiting for transfers between devices  153 us (57%)
  starting transfers between devices  35.1 us (13%)
  local copies, waits for them, and re-layouts  23.6 us (9%)
  Pallas kernels  22 us (8%)
  matrix products  14.3 us (5%)
  between operations  14.3 us (5%)
  other arithmetic  6.51 us (2%)
    psum x1, waiting for transfers between devices, shards(): total = lax.psum(part, 'energy', axis_index_groups=lines)  45.8 us
    ppermute x1, waiting for transfers between devices, shards(): lax.ppermute(chosen(lax.axis_index('energy') + 1 - 2 * column), 'energy',...  32.1 us
    ppermute x2, waiting for transfers between devices, shards(): low.append(lax.ppermute(mine[c][-levels:], 'energy', up))  29.4 us
    all_to_all x2, waiting for transfers between devices, shards(): lax.all_to_all(piece, both, 0, 0, axis_index_groups=groups, tiled=True)  23.4 us
    pallas_call x4, Pallas kernels, tiled(): pl.pallas_call(body, grid=(rows // TILE,), in_specs=[spec(a.shape[0]) for...  22 us
    all_gather x1, waiting for transfers between devices, shards(): lax.all_gather(phonon, 'energy', axis=0, axis_index_groups=lines, tiled=T...  20.8 us
    ppermute x2, starting transfers between devices, shards(): low.append(lax.ppermute(mine[c][-levels:], 'energy', up))  11.1 us
    unnamed x16, local copies, waits for them, and re-layouts  10.6 us
  transfers between devices with their start and end apart: 12, of which 7 were waited for; matrix products, arithmetic and copies ran while one was open for 10% of the time, Pallas kernels for 6%

profile of v4, /device:TPU:0, one launch (start us, length us, event | category | flops | bytes accessed | tf_op | source)
XLA Modules:
  0.0 268.8 jit_solution(6933596859492696870)
XLA Ops:
  7.2 4.1 %fusion.36 = (f32[2,4,2,2,1,64,256]{6,5,4,3,2,1,0:T(8,128)S(1)}, f32[2,4,2,2,1,64,256]{6,5,4,3,2,1,0:T(8,128)}) fusion(f32[2,4,2,2,2,64,256]{6,5,4,3,2,1,0:T(8,128)} %bitcast.84), kind=kLoop, calls=%fused_computation.46 | loop fusion | bytes 8388608 | tf_op jit(solution)/shard_map/slice | solution.py:118
  11.3 1.6 copy.52
  12.8 5.2 %all-to-all-start = ((f32[16,2,64,256]{3,2,1,0:T(8,128)}), f32[16,2,64,256]{3,2,1,0:T(8,128)S(1)}, u32[]{:S(2)}, u32[]{:S(2)}) async-start(f32[16,2,64,256]{3,2,1,0:T(8,128)} %bitcast.81), calls=%async_computation | async-start | bytes 4194304 | tf_op jit(solution)/shard_map/all_to_all | solution.py:121
  18.7 3.1 %copy.51 = f32[2,4,2,2,1,64,256]{6,5,2,0,1,3,4:T(8,128)} copy(f32[2,4,2,2,1,64,256]{6,5,4,3,2,1,0:T(8,128)} %get-tuple-element.29) | data formatting | bytes 4194304
  21.9 21.8 %all-to-all-done.own_ref = f32[16,2,64,256]{3,2,1,0:T(8,128)S(1)} async-done(((f32[16,2,64,256]{3,2,1,0:T(8,128)}), f32[16,2,64,256]{3,2,1,0:T(8,128)S(1)}, u32[]{:S(2)}, u32[]{:S(2)}) %all-to-all-start) | async-done | bytes 2097184 | tf_op jit(solution)/shard_map/all_to_all | solution.py:121
  43.7 4.5 %all-to-all-start.1 = ((f32[16,2,64,256]{3,2,1,0:T(8,128)}), f32[16,2,64,256]{3,2,1,0:T(8,128)}, u32[]{:S(2)}, u32[]{:S(2)}) async-start(f32[16,2,64,256]{3,2,1,0:T(8,128)} %bitcast.80), calls=%async_computation.1 | async-start | bytes 4194304 | tf_op jit(solution)/shard_map/all_to_all | solution.py:121
  48.7 1.6 fusion.37
  51.6 20.8 %all-gather.2.cloned.1.call-done = f32[16,1,2,128,128]{4,3,2,1,0:T(8,128)} async-done(((f32[4,1,2,128,128]{4,3,2,1,0:T(8,128)}), f32[16,1,2,128,128]{4,3,2,1,0:T(8,128)}) %all-gather.2.cloned.1.call-update) | async-done | bytes 2097168 | tf_op jit(solution)/shard_map/all_gather | solution.py:107
  72.4 1.5 all-to-all-done.1.own_ref
  73.9 2.8 %copy.66 = f32[2,8,256,128]{3,1,2,0:T(8,128)S(1)} copy(f32[2,8,256,128]{3,2,1,0:T(8,128)} %bitcast.86) | data formatting | bytes 4194304
  77.1 4.2 %fusion = f32[16,2,128,128]{3,0,2,1:T(8,128)} fusion(f32[16,16,1,1]{0,1,3,2:T(8,128)S(1)} %bitcast.87, f32[2,128,128,16]{2,1,0,3:T(8,128)S(1)} %bitcast.82), kind=kOutput, calls=%fused_computation.4 | convolution fusion | flops 100663296 | bytes 4195328 | tf_op jit(solution)/shard_map/dot_general | solution.py:136
  81.3 1.5 collective-permute-start.4
  82.8 6.1 %collective-permute-start.1 = (f32[8,2,64,256]{3,2,1,0:T(8,128)}, f32[8,2,64,256]{3,2,1,0:T(8,128)}, u32[]{:S(2)}, u32[]{:S(2)}) collective-permute-start(f32[8,2,64,256]{3,2,1,0:T(8,128)} %get-tuple-element.31), channel_id=1, source_target_pairs={{0,8},{4,12},{8,16},{12,20},{16,24},{20,28},{1,9},{5,13},{9,17},{1... | collective-permute-start | bytes 3145736 | tf_op jit(solution)/shard_map/ppermute | solution.py:125
  88.8 3.1 %fusion.38 = (f32[8,2,64,256]{3,2,1,0:T(8,128)}, f32[8,2,64,256]{3,2,1,0:T(8,128)}) fusion(f32[16,2,64,256]{3,2,1,0:T(8,128)} %all-to-all-done.1.own_ref), kind=kLoop, calls=%fused_computation.48 | loop fusion | bytes 4194304 | tf_op jit(solution)/shard_map/slice | solution.py:125
  91.9 5.0 %collective-permute-start.2 = (f32[8,2,64,256]{3,2,1,0:T(8,128)}, f32[8,2,64,256]{3,2,1,0:T(8,128)}, u32[]{:S(2)}, u32[]{:S(2)}) collective-permute-start(f32[8,2,64,256]{3,2,1,0:T(8,128)} %get-tuple-element.32), channel_id=1, source_target_pairs={{0,8},{4,12},{8,16},{12,20},{16,24},{20,28},{1,9},{5,13},{9,17},{1... | collective-permute-start | bytes 3145736 | tf_op jit(solution)/shard_map/ppermute | solution.py:125
  98.4 2.6 shard_map.68
  102.7 9.1 %collective-permute-done.1.low_ref = f32[8,2,64,256]{3,2,1,0:T(8,128)} collective-permute-done((f32[8,2,64,256]{3,2,1,0:T(8,128)}, f32[8,2,64,256]{3,2,1,0:T(8,128)}, u32[]{:S(2)}, u32[]{:S(2)}) %collective-permute-start.1) | collective-permute-done | bytes 1048608 | tf_op jit(solution)/shard_map/ppermute | solution.py:125
  111.7 20.3 %collective-permute-done.2.low_ref = f32[8,2,64,256]{3,2,1,0:T(8,128)} collective-permute-done((f32[8,2,64,256]{3,2,1,0:T(8,128)}, f32[8,2,64,256]{3,2,1,0:T(8,128)}, u32[]{:S(2)}, u32[]{:S(2)}) %collective-permute-start.2) | collective-permute-done | bytes 1048608 | tf_op jit(solution)/shard_map/ppermute | solution.py:125
  132.1 5.5 %shard_map.69 = f32[8,2,64,256]{3,2,1,0:T(8,128)S(1)} custom-call(f32[16,2,64,256]{3,2,1,0:T(8,128)} %all-to-all-done.1.own_ref, f32[8,2,64,256]{3,2,1,0:T(8,128)} %collective-permute-done.high_ref), custom_call_target="tpu_custom_call" | custom-call | flops 16777216 | bytes 4194304 | tf_op jit(solution)/shard_map/pallas_call | solution.py:81
  138.2 2.0 fusion.12
  140.2 2.5 add.63
  145.0 7.2 %shard_map.71 = f32[16,2,64,256]{3,2,1,0:T(8,128)S(1)} custom-call(f32[8,2,64,256]{3,2,1,0:T(8,128)} %collective-permute-done.2.low_ref, f32[16,2,64,256]{3,2,1,0:T(8,128)} %all-to-all-done.1.own_ref, f32[8,2,64,256]{3,2,1,0:T(8,128)} %collective-permute-done.high_ref, f32[16,2,64,256]{3,2,1,0:T(8,128)S(1)} %fusion.13.table_ref), custom_call_target="tpu_custom_call" | custom-call | flops 33554432 | bytes 8388608 | tf_op jit(solution)/shard_map/pallas_call | solution.py:81
  153.5 4.4 %all-to-all-start.3 = ((f32[16,2,64,256]{3,2,1,0:T(8,128)}), f32[16,2,64,256]{3,2,1,0:T(8,128)}, u32[]{:S(2)}, u32[]{:S(2)}) async-start(f32[16,2,64,256]{3,2,1,0:T(8,128)} %copy-done.2), calls=%async_computation.3 | async-start | bytes 4194304 | tf_op jit(solution)/shard_map/all_to_all | solution.py:155
  158.6 2.8 %fusion.6 = f32[16,2,64,128]{3,2,1,0:T(8,128)S(1)} fusion(f32[16,2,128,128]{3,0,2,1:T(8,128)} %copy-done.3, f32[256,128]{1,0:T(8,128)S(1)} %copy-done, s32[]{:T(128)S(6)} %select_n.24), kind=kOutput, calls=%fused_computation.10 | convolution fusion | flops 201326592 | bytes 3178500 | tf_op jit(solution)/shard_map/im,lpmk->lpik/dot_general | solution.py:150
  162.4 6.6 %shard_map.70 = f32[16,2,64,256]{3,2,1,0:T(8,128)S(1)} custom-call(f32[8,2,64,256]{3,2,1,0:T(8,128)} %collective-permute-done.1.low_ref, f32[16,2,64,256]{3,2,1,0:T(8,128)S(1)} %all-to-all-done.own_ref, f32[8,2,64,256]{3,2,1,0:T(8,128)S(1)} %collective-permute-done.3.high_ref, f32[16,2,64,256]{3,2,1,0:T(8,128)S(1)} %fusion.15.table_ref), custom_call_target="tpu_custom_call" | custom-call | flops 33554432 | bytes 8388608 | tf_op jit(solution)/shard_map/pallas_call | solution.py:81
  170.4 45.8 %all-reduce.2.cloned.1.call-done = f32[8,2,128,128]{2,3,1,0:T(8,128)} async-done(((f32[8,2,128,128]{2,3,1,0:T(8,128)}), f32[8,2,128,128]{2,3,1,0:T(8,128)}) %all-reduce.2.cloned.1.call-update) | async-done | bytes 1048592 | tf_op jit(solution)/shard_map/psum | solution.py:146
  216.2 3.7 %all-to-all-start.2 = ((f32[16,2,64,256]{3,2,1,0:T(8,128)}), f32[16,2,64,256]{3,2,1,0:T(8,128)S(1)}, u32[]{:S(2)}, u32[]{:S(2)}) async-start(f32[16,2,64,256]{3,2,1,0:T(8,128)} %copy-done.1), calls=%async_computation.2 | async-start | bytes 4194304 | tf_op jit(solution)/shard_map/all_to_all | solution.py:155
  220.1 1.6 copy.44
  222.6 2.1 collective-permute-start.5
  224.7 32.1 %collective-permute-done.5 = f32[4,2,128,128]{3,2,1,0:T(8,128)S(1)} collective-permute-done((f32[4,2,128,128]{3,2,1,0:T(8,128)S(1)}, f32[4,2,128,128]{3,2,1,0:T(8,128)S(1)}, u32[]{:S(2)}, u32[]{:S(2)}) %collective-permute-start.5) | collective-permute-done | bytes 524320 | tf_op jit(solution)/shard_map/ppermute | solution.py:165
  257.7 1.9 pad_maximum_fusion
  259.6 2.3 copy.43
  (44 shorter events, 15.2 us)
Async XLA Ops:
  7.2 93.9 %copy-start = (f32[256,128]{1,0:T(8,128)S(1)}, f32[256,128]{1,0:T(8,128)}, u32[]{:S(2)}) copy-start(f32[256,128]{1,0:T(8,128)} %param.7) | copy-start | bytes 393220
  12.8 30.9 %all-to-all-start = ((f32[16,2,64,256]{3,2,1,0:T(8,128)}), f32[16,2,64,256]{3,2,1,0:T(8,128)S(1)}, u32[]{:S(2)}, u32[]{:S(2)}) async-start(f32[16,2,64,256]{3,2,1,0:T(8,128)} %bitcast.81), calls=%async_computation | async-start | bytes 4194304 | tf_op jit(solution)/shard_map/all_to_all | solution.py:121
  18.0 54.4 %all-gather.2.cloned.1.call-start = ((), (), s32[]{:S(2)}) async-start(), calls=%async_computation.4 | async-start | bytes 2621440 | tf_op jit(solution)/shard_map/all_gather | solution.py:107
  43.7 4.5 %copy-start.5 = (f32[32]{0:T(128)S(1)}, f32[32]{0:T(128)}, u32[]{:S(2)}) copy-start(f32[32]{0:T(128)} %param.8) | copy-start | bytes 388
  43.7 4.7 %copy-start.4 = (s32[32]{0:T(128)S(1)}, s32[32]{0:T(128)}, u32[]{:S(2)}) copy-start(s32[32]{0:T(128)} %param.9) | copy-start | bytes 388
  43.7 30.2 %all-to-all-start.1 = ((f32[16,2,64,256]{3,2,1,0:T(8,128)}), f32[16,2,64,256]{3,2,1,0:T(8,128)}, u32[]{:S(2)}, u32[]{:S(2)}) async-start(f32[16,2,64,256]{3,2,1,0:T(8,128)} %bitcast.80), calls=%async_computation.1 | async-start | bytes 4194304 | tf_op jit(solution)/shard_map/all_to_all | solution.py:121
  50.3 48.1 %collective-permute-start.3 = (f32[8,2,64,256]{3,2,1,0:T(8,128)}, f32[8,2,64,256]{3,2,1,0:T(8,128)S(1)}, u32[]{:S(2)}, u32[]{:S(2)}) collective-permute-start(f32[8,2,64,256]{3,2,1,0:T(8,128)} %get-tuple-element.30), channel_id=1, source_target_pairs={{8,0},{12,4},{16,8},{20,12},{24,16},{28,20},{9,1},{13,5},{17,9},{2... | collective-permute-start | bytes 3145736 | tf_op jit(solution)/shard_map/ppermute | solution.py:124
  81.3 58.9 %collective-permute-start.4 = (f32[16,2,128,128]{3,0,2,1:T(8,128)}, f32[16,2,128,128]{3,0,2,1:T(8,128)}, u32[]{:S(2)}, u32[]{:S(2)}) collective-permute-start(f32[16,2,128,128]{3,0,2,1:T(8,128)} %fusion), channel_id=1, source_target_pairs={{0,4},{4,0},{8,12},{12,8},{16,20},{20,16},{24,28},{28,24},{1,5},{5... | collective-permute-start | bytes 6291464 | tf_op jit(solution)/shard_map/ppermute | solution.py:139
  82.8 29.0 %collective-permute-start.1 = (f32[8,2,64,256]{3,2,1,0:T(8,128)}, f32[8,2,64,256]{3,2,1,0:T(8,128)}, u32[]{:S(2)}, u32[]{:S(2)}) collective-permute-start(f32[8,2,64,256]{3,2,1,0:T(8,128)} %get-tuple-element.31), channel_id=1, source_target_pairs={{0,8},{4,12},{8,16},{12,20},{16,24},{20,28},{1,9},{5,13},{9,17},{1... | collective-permute-start | bytes 3145736 | tf_op jit(solution)/shard_map/ppermute | solution.py:125
  91.9 40.1 %collective-permute-start.2 = (f32[8,2,64,256]{3,2,1,0:T(8,128)}, f32[8,2,64,256]{3,2,1,0:T(8,128)}, u32[]{:S(2)}, u32[]{:S(2)}) collective-permute-start(f32[8,2,64,256]{3,2,1,0:T(8,128)} %get-tuple-element.32), channel_id=1, source_target_pairs={{0,8},{4,12},{8,16},{12,20},{16,24},{20,28},{1,9},{5,13},{9,17},{1... | collective-permute-start | bytes 3145736 | tf_op jit(solution)/shard_map/ppermute | solution.py:125
  96.9 35.1 %collective-permute-start = (f32[8,2,64,256]{3,2,1,0:T(8,128)}, f32[8,2,64,256]{3,2,1,0:T(8,128)}, u32[]{:S(2)}, u32[]{:S(2)}) collective-permute-start(f32[8,2,64,256]{3,2,1,0:T(8,128)} %get-tuple-element.33), channel_id=1, source_target_pairs={{8,0},{12,4},{16,8},{20,12},{24,16},{28,20},{9,1},{13,5},{17,9},{2... | collective-permute-start | bytes 3145736 | tf_op jit(solution)/shard_map/ppermute | solution.py:124
  142.6 1.3 copy-start.3
  152.2 1.3 copy-start.2
  153.5 62.7 %all-to-all-start.3 = ((f32[16,2,64,256]{3,2,1,0:T(8,128)}), f32[16,2,64,256]{3,2,1,0:T(8,128)}, u32[]{:S(2)}, u32[]{:S(2)}) async-start(f32[16,2,64,256]{3,2,1,0:T(8,128)} %copy-done.2), calls=%async_computation.3 | async-start | bytes 4194304 | tf_op jit(solution)/shard_map/all_to_all | solution.py:155
  157.9 58.4 %all-reduce.2.cloned.1.call-start = ((), (), s32[]{:S(2)}) async-start(), calls=%async_computation.5 | async-start | bytes 2097152 | tf_op jit(solution)/shard_map/psum | solution.py:146
  169.1 1.3 copy-start.1
  216.2 41.5 %all-to-all-start.2 = ((f32[16,2,64,256]{3,2,1,0:T(8,128)}), f32[16,2,64,256]{3,2,1,0:T(8,128)S(1)}, u32[]{:S(2)}, u32[]{:S(2)}) async-start(f32[16,2,64,256]{3,2,1,0:T(8,128)} %copy-done.1), calls=%async_computation.2 | async-start | bytes 4194304 | tf_op jit(solution)/shard_map/all_to_all | solution.py:155
  222.6 34.2 %collective-permute-start.5 = (f32[4,2,128,128]{3,2,1,0:T(8,128)S(1)}, f32[4,2,128,128]{3,2,1,0:T(8,128)S(1)}, u32[]{:S(2)}, u32[]{:S(2)}) collective-permute-start(f32[4,2,128,128]{3,2,1,0:T(8,128)S(1)} %get-tuple-element.26), channel_id=1, source_target_pairs={{0,4},{4,0},{8,12},{12,8},{16,20},{20,16},{24,28},{28,24},{1,5},{5... | collective-permute-start | bytes 1572872 | tf_op jit(solution)/shard_map/ppermute | solution.py:165
Sparse Core Ops, SparseCore 0:
  20.4 51.9 all-gather.1
  161.1 55.0 all-reduce.1
